TPU v7x, 32 devices: a whole 2x2x4 slice. The times are simulated.
32 devices in a mesh: fsdp: 4 (over z), seq: 8 (over y, x, core).
Axes of the slice: x: 2, y: 2, z: 4, core: 2. Of those that a mesh axis runs over, the one named last changes fastest.
Arguments:
- queries: bfloat16 [4, 2048, 2048], P('fsdp', 'seq'), may hold values from -32 to 32
- keys: bfloat16 [4, 2048, 2048], P('fsdp', 'seq'), may hold values from -6 to 6
- values: bfloat16 [4, 2048, 2048], P('fsdp', 'seq'), may hold values from -6 to 6
- out_grad: bfloat16 [4, 2048, 2048], P('fsdp', 'seq'), may hold values from -6 to 6
- out_weight: bfloat16 [2048, 2048], P('fsdp'), may hold values from -0.125 to 0.125
- key_blocks: int32 [4, 16, 10], P('fsdp'), may hold values from 0 to 15, as said below
- block_counts: int32 [4, 16], P('fsdp'), may hold values from 2 to 10, as said below
Outputs:
- query_grad: bfloat16 [4, 2048, 2048], P('fsdp', 'seq')
- key_grad: bfloat16 [4, 2048, 2048], P('fsdp', 'seq')
- value_grad: bfloat16 [4, 2048, 2048], P('fsdp', 'seq')
- wo_grad: float32 [2048, 2048], P('fsdp')
Inputs may be any that keep to these rules, and one draw needn't show every extreme that they name: `key_blocks`: within a row the numbers are distinct; slots 0, 1 and 2 hold blocks i, i + 1 and i - 1 modulo 16; slots at or past the row's count are ignored. `block_counts`: every sample has a query block whose count is 10.
All inputs are finite; a program needn't handle non-finite values.
Results may differ from a plain program's by a relative error of at most 0.025.
Values may be sent and summed in bfloat16 or wider, within the bound.
No kernel may reach another device: no remote copies, remote signals or barrier semaphores. Data moves between devices by JAX's collectives and lax.ppermute only.
A program may use at most 128 MiB of HBM per device.

v0:
```python
import jax
import jax.numpy as jnp
from jax import lax
from jax.sharding import PartitionSpec as P

HEADS = 32
HD = 64
BLK = 128
MAXK = 10


NEG_FILL = -1e30


def pair_scores(query_blocks, chosen):
    return jnp.einsum(
        "iqhd,ikhd->ihqk", query_blocks, chosen, preferred_element_type=jnp.float32
    ) * HD ** (-0.5)


def blocked(array):
    return array.reshape(-1, BLK, array.shape[1], HD)


def head_forward(query_h, key_h, value_h, adjacency, slot_live):
    query_blocks = blocked(query_h)
    key_heads = blocked(key_h)
    value_heads = blocked(value_h)
    blocks_total = query_blocks.shape[0]
    head_count = query_blocks.shape[2]

    def stat_step(carried, slot):
        row_max, row_sum = carried
        score = pair_scores(query_blocks, key_heads[adjacency[:, slot]])
        usable = slot_live[:, slot][:, None, None, None]
        score = jnp.where(usable, score, NEG_FILL)
        new_max = jnp.maximum(row_max, jnp.max(score, axis=-1))
        expo = jnp.where(usable, jnp.exp(score - new_max[..., None]), 0.0)
        row_sum = row_sum * jnp.exp(row_max - new_max) + jnp.sum(expo, axis=-1)
        return ((new_max, row_sum), None)

    start_max = jnp.full((blocks_total, head_count, BLK), NEG_FILL, jnp.float32)
    start_sum = jnp.zeros((blocks_total, head_count, BLK), jnp.float32)
    (row_max, row_sum), _ = lax.scan(stat_step, (start_max, start_sum), jnp.arange(MAXK))

    def output_step(accum, slot):
        picked = adjacency[:, slot]
        score = pair_scores(query_blocks, key_heads[picked])
        usable = slot_live[:, slot][:, None, None, None]
        prob_half = jnp.where(
            usable, jnp.exp(score - row_max[..., None]) / row_sum[..., None], 0.0
        ).astype(jnp.bfloat16)
        accum = accum + jnp.einsum(
            "ihqk,ikhd->iqhd", prob_half, value_heads[picked], preferred_element_type=jnp.float32
        )
        return (accum, None)

    start_out = jnp.zeros(query_blocks.shape, jnp.float32)
    accum, _ = lax.scan(output_step, start_out, jnp.arange(MAXK))
    return (row_max, row_sum, accum.astype(jnp.bfloat16))


def head_backward(
    query_h, key_h, value_h, grad_h, row_max, row_sum, attn_blocks, adjacency, slot_live
):
    query_blocks = blocked(query_h)
    key_heads = blocked(key_h)
    value_heads = blocked(value_h)
    grad_blocks = blocked(grad_h)
    scale_factor = HD ** (-0.5)
    row_dot = jnp.sum(
        grad_blocks.astype(jnp.float32) * attn_blocks.astype(jnp.float32), axis=-1
    ).transpose(0, 2, 1)

    def grad_step(carried, slot):
        query_accum, key_accum, value_accum = carried
        picked = adjacency[:, slot]
        chosen_keys = key_heads[picked]
        chosen_values = value_heads[picked]
        score = pair_scores(query_blocks, chosen_keys)
        usable = slot_live[:, slot][:, None, None, None]
        prob_full = jnp.where(usable, jnp.exp(score - row_max[..., None]) / row_sum[..., None], 0.0)
        prob_half = prob_full.astype(jnp.bfloat16)
        prob_grad = jnp.einsum(
            "iqhd,ikhd->ihqk", grad_blocks, chosen_values, preferred_element_type=jnp.float32
        )
        score_grad = (prob_full * (prob_grad - row_dot[..., None])).astype(jnp.bfloat16)
        query_accum = (
            query_accum
            + jnp.einsum(
                "ihqk,ikhd->iqhd", score_grad, chosen_keys, preferred_element_type=jnp.float32
            )
            * scale_factor
        )
        key_terms = (
            jnp.einsum(
                "ihqk,iqhd->ikhd", score_grad, query_blocks, preferred_element_type=jnp.float32
            )
            * scale_factor
        )
        value_terms = jnp.einsum(
            "ihqk,iqhd->ikhd", prob_half, grad_blocks, preferred_element_type=jnp.float32
        )
        key_accum = key_accum.at[picked].add(key_terms)
        value_accum = value_accum.at[picked].add(value_terms)
        return ((query_accum, key_accum, value_accum), None)

    zeros_start = jnp.zeros(query_blocks.shape, jnp.float32)
    (query_accum, key_accum, value_accum), _ = lax.scan(
        grad_step, (zeros_start, zeros_start, zeros_start), jnp.arange(MAXK)
    )
    head_count = query_h.shape[1]
    return tuple(
        (
            accum.astype(jnp.bfloat16).reshape(-1, head_count, HD)
            for accum in (query_accum, key_accum, value_accum)
        )
    )


def on_device(queries, keys, values, out_grad, out_weight, key_blocks, block_counts):
    local_tokens = queries.shape[1]
    model_width = queries.shape[2]
    seq_devices = lax.axis_size("seq")
    loss_grad = out_grad[0]
    adjacency = key_blocks[0]
    slot_live = jnp.arange(MAXK)[None, :] < block_counts[0][:, None]

    def head_groups(array):
        return array[0].reshape(local_tokens, seq_devices, HEADS // seq_devices, HD)

    attn_grad = lax.dot_general(
        loss_grad,
        lax.all_gather(out_weight, "fsdp", axis=0, tiled=True),
        (((1,), (1,)), ((), ())),
        preferred_element_type=jnp.float32,
    ).astype(jnp.bfloat16)

    def attend(heads_in):
        query_h, key_h, value_h, grad_h = (member[:, 0] for member in heads_in)
        row_max, row_sum, attn_blocks = head_forward(query_h, key_h, value_h, adjacency, slot_live)
        query_g, key_g, value_g = head_backward(
            query_h, key_h, value_h, grad_h, row_max, row_sum, attn_blocks, adjacency, slot_live
        )
        return (query_g, key_g, value_g, attn_blocks.reshape(-1, query_h.shape[1], HD))

    query_g, key_g, value_g, attn_heads = attend(
        (
            lax.all_to_all(head_groups(queries), "seq", split_axis=1, concat_axis=0, tiled=True),
            lax.all_to_all(head_groups(keys), "seq", split_axis=1, concat_axis=0, tiled=True),
            lax.all_to_all(head_groups(values), "seq", split_axis=1, concat_axis=0, tiled=True),
            lax.all_to_all(
                head_groups(attn_grad[None]), "seq", split_axis=1, concat_axis=0, tiled=True
            ),
        )
    )
    query_t, key_t, value_t, attn_t = (
        lax.all_to_all(query_g, "seq", split_axis=0, concat_axis=1, tiled=True),
        lax.all_to_all(key_g, "seq", split_axis=0, concat_axis=1, tiled=True),
        lax.all_to_all(value_g, "seq", split_axis=0, concat_axis=1, tiled=True),
        lax.all_to_all(attn_heads, "seq", split_axis=0, concat_axis=1, tiled=True),
    )
    attn_out = attn_t.reshape(local_tokens, model_width)
    share = lax.psum_scatter(
        lax.dot_general(
            attn_out, loss_grad, (((0,), (0,)), ((), ())), preferred_element_type=jnp.float32
        ),
        ("fsdp", "seq"),
        scatter_dimension=0,
        tiled=True,
    )
    wo_grad = lax.all_gather(share.astype(jnp.bfloat16), "seq", axis=0, tiled=True).astype(
        share.dtype
    )

    def to_tokens(array):
        return array.reshape(1, local_tokens, model_width)

    return (to_tokens(query_t), to_tokens(key_t), to_tokens(value_t), wo_grad)


def solution(mesh):
    return jax.shard_map(
        on_device,
        mesh=mesh,
        in_specs=(
            P("fsdp", "seq", None),
            P("fsdp", "seq", None),
            P("fsdp", "seq", None),
            P("fsdp", "seq", None),
            P("fsdp", None),
            P("fsdp", None, None),
            P("fsdp", None),
        ),
        out_specs=(
            P("fsdp", "seq", None),
            P("fsdp", "seq", None),
            P("fsdp", "seq", None),
            P("fsdp", None),
        ),
        check_vma=False,
    )
```

profile of v0, /device:TPU:16, one launch (start us, length us, event | category | flops | bytes accessed | tf_op | source)
XLA Modules:
  0.0 1125.7 jit_solution(12596100546542482886)
XLA Ops:
  14.6 14.1 %all-to-all-done.1 = bf16[256,8,4,64]{0,3,2,1:T(8,128)(2,1)S(1)} async-done(((bf16[256,8,4,64]{0,3,2,1:T(8,128)(2,1)}), bf16[256,8,4,64]{0,3,2,1:T(8,128)(2,1)S(1)}, u32[]{:S(2)}, u32[]{:S(2)}) %all-to-all-start.1) | async-done | bytes 1048608 | tf_op jit(solution)/shard_map/all_to_all | solution.py:149
  34.6 13.1 %all-to-all-done = bf16[256,8,4,64]{0,3,2,1:T(8,128)(2,1)S(1)} async-done(((bf16[256,8,4,64]{0,3,2,1:T(8,128)(2,1)}), bf16[256,8,4,64]{0,3,2,1:T(8,128)(2,1)S(1)}, u32[]{:S(2)}, u32[]{:S(2)}) %all-to-all-start) | async-done | bytes 1048608 | tf_op jit(solution)/shard_map/all_to_all | solution.py:150
  57.9 9.5 all-to-all-done.2
  71.5 105.4 %while.39 = (s32[]{:T(128)}, f32[16,4,128]{2,1,0:T(4,128)S(1)}, f32[16,4,128]{2,1,0:T(4,128)S(1)}, s32[10]{0:T(128)S(1)}, pred[16,10]{0,1:T(8,128)(4,1)S(1)}, /*...) while((s32[]{:T(128)}, f32[16,4,128]{2,1,0:T(4,128)S(1)}, ...), condition=%wide.region_3.4_spmd.clone, body=%wide.region_0.3_spmd.clone.sunk | while | flops 142648368 | bytes 13013494 | solution.py:44
  176.9 26.8 %all-gather.3.cloned.1.call-done = bf16[2048,2048]{1,0:T(8,128)(2,1)} async-done(((bf16[512,2048]{1,0:T(8,128)(2,1)}), bf16[2048,2048]{1,0:T(8,128)(2,1)}) %all-gather.3.cloned.1.call-update) | async-done | bytes 8388624 | tf_op jit(solution)/shard_map/all_gather | solution.py:134
  203.8 6.7 convolution_convert_fusion
  217.2 172.3 %while.40 = (s32[]{:T(128)}, f32[16,128,4,64]{1,3,2,0:T(8,128)}, s32[10]{0:T(128)S(1)}, s32[16,10]{0,1:T(8,128)S(1)}, bf16[16,128,4,64]{3,2,1,0:T(4,128)(2,1)}, ...) while((s32[]{:T(128)}, f32[16,128,4,64]{1,3,2,0:T(8,128)}, ...), condition=%wide.region_5.6_spmd.clone, body=%wide.region_4.5_spmd.clone.sunk | while | flops 274728000 | bytes 11604533 | solution.py:59
  245.1 6.0 bitcast_add_fusion.4
  262.4 6.0 bitcast_add_fusion.4
  279.7 6.0 bitcast_add_fusion.4
  297.0 6.0 bitcast_add_fusion.4
  314.3 6.0 bitcast_add_fusion.4
  331.6 6.0 bitcast_add_fusion.4
  348.9 6.0 bitcast_add_fusion.4
  366.2 6.0 bitcast_add_fusion.4
  383.5 6.0 bitcast_add_fusion.4
  406.5 19.6 %all_to_all.120 = bf16[8,2,32768]{2,1,0:T(2,128)(2,1)} all-to-all(bf16[8,2,32768]{2,1,0:T(2,128)(2,1)} %reshape.137), channel_id=1, replica_groups=mesh['fsdp'=4,'seq'=8] {'seq'}, dimensions={0} | all-to-all | bytes 2097152 | tf_op jit(solution)/shard_map/all_to_all | solution.py:161
  434.3 9.3 fusion.24
  445.5 177.9 %reduce-scatter.2.cloned.1.call-done = f32[64,2048]{1,0:T(8,128)} async-done(((f32[2048,2048]{1,0:T(8,128)}), f32[64,2048]{1,0:T(8,128)}) %reduce-scatter.2.cloned.1.call-update) | async-done | bytes 524304 | tf_op jit(solution)/shard_map/reduce_scatter | solution.py:164
  628.3 413.4 %while.41 = (s32[]{:T(128)}, f32[16,128,4,64]{1,3,2,0:T(8,128)}, f32[16,128,4,64]{1,3,2,0:T(8,128)}, f32[16,128,4,64]{1,3,2,0:T(8,128)}, s32[10]{0:T(128)S(1)}, ...) while((s32[]{:T(128)}, f32[16,128,4,64]{1,3,2,0:T(8,128)}, ...), condition=%wide.region_10.11_spmd.clone, body=%wide.region_7.10_spmd.clone.sunk | while | flops 682624064 | bytes 70357800 | solution.py:109
  651.7 5.4 scatter_fusion.1
  1050.5 6.2 all-to-all-start.6
  1063.8 8.3 all-to-all-done.6
  1080.6 11.2 all-to-all-done.4
  (440 shorter events, 689.3 us)
Async XLA Ops:
  7.2 196.6 %copy-start = (bf16[1,256,2048]{2,1,0:T(8,128)(2,1)S(1)}, bf16[1,256,2048]{2,1,0:T(8,128)(2,1)}, u32[]{:S(2)}) copy-start(bf16[1,256,2048]{2,1,0:T(8,128)(2,1)} %param.16) | copy-start | bytes 3145732
  7.2 6.1 copy-start.8
  9.6 19.1 %all-to-all-start.1 = ((bf16[256,8,4,64]{0,3,2,1:T(8,128)(2,1)}), bf16[256,8,4,64]{0,3,2,1:T(8,128)(2,1)S(1)}, u32[]{:S(2)}, u32[]{:S(2)}) async-start(bf16[256,8,4,64]{0,3,2,1:T(8,128)(2,1)} %bitcast.4), calls=%async_computation.1 | async-start | bytes 2097152 | tf_op jit(solution)/shard_map/all_to_all | solution.py:149
  28.7 18.9 %all-to-all-start = ((bf16[256,8,4,64]{0,3,2,1:T(8,128)(2,1)}), bf16[256,8,4,64]{0,3,2,1:T(8,128)(2,1)S(1)}, u32[]{:S(2)}, u32[]{:S(2)}) async-start(bf16[256,8,4,64]{0,3,2,1:T(8,128)(2,1)} %bitcast.172), calls=%async_computation | async-start | bytes 2097152 | tf_op jit(solution)/shard_map/all_to_all | solution.py:150
  47.6 5.1 copy-start.7
  47.6 5.2 copy-start.9
  47.6 5.2 copy-start.10
  47.6 19.8 %all-to-all-start.2 = ((bf16[256,8,4,64]{0,3,2,1:T(8,128)(2,1)}), bf16[256,8,4,64]{0,3,2,1:T(8,128)(2,1)}, u32[]{:S(2)}, u32[]{:S(2)}) async-start(bf16[256,8,4,64]{0,3,2,1:T(8,128)(2,1)} %bitcast.171), calls=%async_computation.2 | async-start | bytes 2097152 | tf_op jit(solution)/shard_map/all_to_all | solution.py:151
  52.0 151.7 %all-gather.3.cloned.1.call-start = ((), (), s32[]{:S(2)}) async-start(), calls=%async_computation.9 | async-start | bytes 10485760 | tf_op jit(solution)/shard_map/all_gather | solution.py:134
  212.8 176.7 %all-to-all-start.3 = ((bf16[256,8,4,64]{0,3,2,1:T(8,128)(2,1)}), bf16[256,8,4,64]{0,3,2,1:T(8,128)(2,1)}, u32[]{:S(2)}, u32[]{:S(2)}) async-start(bf16[256,8,4,64]{0,3,2,1:T(8,128)(2,1)} %bitcast.169), calls=%async_computation.3 | async-start | bytes 2097152 | tf_op jit(solution)/shard_map/all_to_all | solution.py:152
  217.0 406.3 %reduce-scatter.2.cloned.1.call-start = ((), (), s32[]{:S(2)}) async-start(), calls=%async_computation.10 | async-start | bytes 17301504 | tf_op jit(solution)/shard_map/reduce_scatter | solution.py:164
  443.7 670.9 %all-gather.5.cloned.1.call-start = ((), (), s32[]{:S(2)}) async-start(), calls=%async_computation.11 | async-start | bytes 2359296 | tf_op jit(solution)/shard_map/all_gather | solution.py:172
  740.0 4.7 copy-start.2
  740.0 4.7 copy-start.6
  864.1 4.7 copy-start.2
  864.1 4.7 copy-start.6
  905.3 4.7 copy-start.6
  946.4 4.7 copy-start.6
  1046.0 10.6 copy-start.5
  1050.5 21.7 %all-to-all-start.6 = ((bf16[8,2,32768]{2,1,0:T(2,128)(2,1)}), bf16[8,2,32768]{2,1,0:T(2,128)(2,1)}, u32[]{:S(2)}, u32[]{:S(2)}) async-start(bf16[8,2,32768]{2,1,0:T(2,128)(2,1)} %reshape.135), calls=%async_computation.6 | async-start | bytes 2097152 | tf_op jit(solution)/shard_map/all_to_all | solution.py:160
  1059.3 17.1 %copy-start.3 = (f32[16,128,4,64]{1,3,2,0:T(8,128)S(1)}, f32[16,128,4,64]{1,3,2,0:T(8,128)}, u32[]{:S(2)}) copy-start(f32[16,128,4,64]{1,3,2,0:T(8,128)} %get-tuple-element.177) | copy-start | bytes 6291460
  1072.1 19.7 %all-to-all-start.4 = ((bf16[8,2,32768]{2,1,0:T(2,128)(2,1)}), bf16[8,2,32768]{2,1,0:T(2,128)(2,1)}, u32[]{:S(2)}, u32[]{:S(2)}) async-start(bf16[8,2,32768]{2,1,0:T(2,128)(2,1)} %reshape.131), calls=%async_computation.4 | async-start | bytes 2097152 | tf_op jit(solution)/shard_map/all_to_all | solution.py:158
  1091.8 18.9 %all-to-all-start.5 = ((bf16[8,2,32768]{2,1,0:T(2,128)(2,1)}), bf16[8,2,32768]{2,1,0:T(2,128)(2,1)S(1)}, u32[]{:S(2)}, u32[]{:S(2)}) async-start(bf16[8,2,32768]{2,1,0:T(2,128)(2,1)} %reshape.133), calls=%async_computation.5 | async-start | bytes 2097152 | tf_op jit(solution)/shard_map/all_to_all | solution.py:159
  1113.2 5.6 copy-start.1
  (24 other events, 95.0 us)
Sparse Core Ops, SparseCore 0:
  54.4 149.2 all-gather.2
  443.8 179.5 reduce-scatter.1
  625.3 30.9 all-gather.4
where the time goes:
time: 1140 us; the launch traced here: 1130 us
  local copies, waits for them, and re-layouts  349 us (31%)
  waiting for transfers between devices  262 us (23%)
  matrix products  258 us (23%)
  other arithmetic  133 us (12%)
  loops' own time  59.5 us (5%)
  starting transfers between devices  30.4 us (3%)
  blocking collectives  19.6 us (2%)
  between operations  14.5 us (1%)
    reduce_scatter x1, waiting for transfers between devices, on_device(): lax.psum_scatter(lax.dot_general(attn_out, loss_grad, (((0,), (0,)), ((),...  178 us
    gather x20, local copies, waits for them, and re-layouts, grad_step(): chosen_keys = key_heads[picked]  75.4 us
    dot_general x10, matrix products, output_step(): jnp.einsum('ihqk,ikhd->iqhd', prob_half, value_heads[picked], preferred_e...  59.6 us
    dot_general x20, matrix products, pair_scores(): jnp.einsum('iqhd,ikhd->ihqk', query_blocks, chosen, preferred_element_typ...  56.9 us
    scatter-add x10, other arithmetic, grad_step(): value_accum = value_accum.at[picked].add(value_terms)  52 us
    gather x10, local copies, waits for them, and re-layouts, grad_step(): chosen_values = value_heads[picked]  51.9 us
    scatter-add x10, other arithmetic, grad_step(): key_accum = key_accum.at[picked].add(key_terms)  51.8 us
    gather x10, local copies, waits for them, and re-layouts, output_step(): value_heads[picked]  51.5 us
  transfers between devices with their start and end apart: 10, of which 8 were waited for; matrix products, arithmetic and copies ran while one was open for 61% of the time, Pallas kernels for 0%

commit v1 on v0

--- a/solution.py
+++ b/solution.py
@@ -1,6 +1,10 @@
+import math
+
 import jax
 import jax.numpy as jnp
 from jax import lax
+from jax.experimental import pallas as pl
+from jax.experimental.pallas import tpu as pltpu
 from jax.sharding import PartitionSpec as P
 
 HEADS = 32
@@ -118,6 +122,149 @@
     )
 
 
+PAIR = 2 * HD
+SCALE = HD ** (-0.5)
+
+
+def fold_rows(tile, combine):
+    return combine(tile.reshape(-1, 8, tile.shape[1]), axis=0)
+
+
+def by_head(block):
+    first = lax.broadcasted_iota(jnp.int32, block.shape, 1) < HD
+    zero = jnp.zeros_like(block)
+    return jnp.concatenate([jnp.where(first, block, zero), jnp.where(first, zero, block)], axis=0)
+
+
+def own_parts(wide):
+    return jnp.concatenate([wide[:HD, :BLK], wide[HD:, BLK:]], axis=0)
+
+
+def dot(left, right, dims=(((1,), (0,)), ((), ()))):
+    return lax.dot_general(left, right, dims, preferred_element_type=jnp.float32)
+
+
+TRANSPOSED = (((1,), (1,)), ((), ()))
+
+
+def attend_kernel(
+    adjacency, counts, query, key, value, grad, query_g, key_g, value_g, attn_out,
+    key_t, value_t, key_sum, value_sum, prob, half, score_g,
+):
+    blocks = query.shape[0] // BLK
+
+    def rows(index):
+        return pl.ds(pl.multiple_of(index * BLK, BLK), BLK)
+
+    @pl.loop(0, blocks)
+    def _(index):
+        key_t[index] = key[rows(index), :].T
+        value_t[index] = value[rows(index), :].T
+        key_sum[rows(index), :] = jnp.zeros((BLK, PAIR), jnp.float32)
+        value_sum[rows(index), :] = jnp.zeros((BLK, PAIR), jnp.float32)
+
+    def query_block(index, slots):
+        live = counts[index]
+        picked = [adjacency[index, slot] for slot in range(slots)]
+        queries = by_head(query[rows(index), :])
+        grad_block = grad[rows(index), :]
+        grads = by_head(grad_block)
+
+        row_max = jnp.full((8, 2 * BLK), NEG_FILL, jnp.float32)
+        for slot in range(slots):
+            score = dot(key[rows(picked[slot]), :], queries, TRANSPOSED)
+            if slot == slots - 1:
+                score = jnp.where(slot < live, score, NEG_FILL)
+            prob[slot] = score
+            row_max = jnp.maximum(row_max, fold_rows(score, jnp.max))
+        row_max = jnp.max(row_max, axis=0, keepdims=True)
+
+        row_sum = jnp.zeros((8, 2 * BLK), jnp.float32)
+        for slot in range(slots):
+            expo = jnp.exp2((prob[slot] - row_max) * (SCALE * math.log2(math.e)))
+            prob[slot] = expo
+            row_sum = row_sum + fold_rows(expo, jnp.sum)
+        inverse = 1.0 / jnp.sum(row_sum, axis=0, keepdims=True)
+
+        for slot in range(slots):
+            full = prob[slot] * inverse
+            prob[slot] = full
+            half[rows(slot), :] = full.astype(jnp.bfloat16)
+
+        out_t = jnp.zeros((PAIR, 2 * BLK), jnp.float32)
+        for slot in range(0, slots, 2):
+            out_t = out_t + dot(
+                jnp.concatenate([value_t[picked[slot]], value_t[picked[slot + 1]]], axis=1),
+                half[pl.ds(slot * BLK, 2 * BLK), :],
+            )
+        out_t = own_parts(out_t).astype(jnp.bfloat16).astype(jnp.float32)
+        attn_out[rows(index), :] = out_t.T.astype(jnp.bfloat16)
+        products = grad_block.astype(jnp.float32).T * out_t
+        row_dot = jnp.concatenate(
+            [
+                jnp.sum(products[:HD], axis=0, keepdims=True),
+                jnp.sum(products[HD:], axis=0, keepdims=True),
+            ],
+            axis=1,
+        )
+
+        for slot in range(slots):
+            prob_grad = dot(value[rows(picked[slot]), :], grads, TRANSPOSED)
+            term = (prob[slot] * (prob_grad - row_dot)).astype(jnp.bfloat16)
+            score_g[rows(slot), :] = term
+            key_sum[rows(picked[slot]), :] += dot(term, queries)
+            value_sum[rows(picked[slot]), :] += dot(half[rows(slot), :], grads)
+
+        query_t = jnp.zeros((PAIR, 2 * BLK), jnp.float32)
+        for slot in range(0, slots, 2):
+            query_t = query_t + dot(
+                jnp.concatenate([key_t[picked[slot]], key_t[picked[slot + 1]]], axis=1),
+                score_g[pl.ds(slot * BLK, 2 * BLK), :],
+            )
+        query_g[rows(index), :] = (own_parts(query_t).T * SCALE).astype(jnp.bfloat16)
+
+    @pl.loop(0, blocks)
+    def _(index):
+        for slots in range(2, MAXK + 1, 2):
+            @pl.when((counts[index] + 1) // 2 == slots // 2)
+            def _():
+                query_block(index, slots)
+
+    key_g[...] = (key_sum[...] * SCALE).astype(jnp.bfloat16)
+    value_g[...] = value_sum[...].astype(jnp.bfloat16)
+
+
+def attend(query, key, value, grad, adjacency, counts):
+    tokens, width = query.shape
+    blocks = tokens // BLK
+    pair = pl.BlockSpec((tokens, PAIR), lambda step: (0, step))
+    scalars = pl.BlockSpec(memory_space=pltpu.SMEM)
+    tiles = width // PAIR * blocks * MAXK
+    return pl.pallas_call(
+        attend_kernel,
+        grid=(width // PAIR,),
+        in_specs=[scalars, scalars] + [pair] * 4,
+        out_specs=[pair] * 4,
+        out_shape=[jax.ShapeDtypeStruct((tokens, width), jnp.bfloat16)] * 4,
+        scratch_shapes=[
+            pltpu.VMEM((blocks, PAIR, BLK), jnp.bfloat16),
+            pltpu.VMEM((blocks, PAIR, BLK), jnp.bfloat16),
+            pltpu.VMEM((tokens, PAIR), jnp.float32),
+            pltpu.VMEM((tokens, PAIR), jnp.float32),
+            pltpu.VMEM((MAXK, BLK, 2 * BLK), jnp.float32),
+            pltpu.VMEM((MAXK * BLK, 2 * BLK), jnp.bfloat16),
+            pltpu.VMEM((MAXK * BLK, 2 * BLK), jnp.bfloat16),
+        ],
+        compiler_params=pltpu.CompilerParams(vmem_limit_bytes=48 * 2**20),
+        cost_estimate=pl.CostEstimate(
+            flops=tiles * 2 * 6 * 2 * BLK * BLK * HD,
+            bytes_accessed=8 * 2 * tokens * width,
+            transcendentals=tiles * 2 * BLK * BLK,
+        ),
+        name="attend",
+    )(adjacency, counts, query, key, value, grad)
+
+
 def on_device(queries, keys, values, out_grad, out_weight, key_blocks, block_counts):
     local_tokens = queries.shape[1]
     model_width = queries.shape[2]
@@ -136,7 +283,11 @@
         preferred_element_type=jnp.float32,
     ).astype(jnp.bfloat16)
 
-    def attend(heads_in):
+    def attend_heads(heads_in):
+        if HEADS // seq_devices % 2 == 0:
+            flat = (member.reshape(-1, HEADS // seq_devices * HD) for member in heads_in)
+            results = attend(*flat, adjacency, block_counts[0])
+            return tuple(result.reshape(-1, HEADS // seq_devices, HD) for result in results)
         query_h, key_h, value_h, grad_h = (member[:, 0] for member in heads_in)
         row_max, row_sum, attn_blocks = head_forward(query_h, key_h, value_h, adjacency, slot_live)
         query_g, key_g, value_g = head_backward(
@@ -144,7 +295,7 @@
         )
         return (query_g, key_g, value_g, attn_blocks.reshape(-1, query_h.shape[1], HD))
 
-    query_g, key_g, value_g, attn_heads = attend(
+    query_g, key_g, value_g, attn_heads = attend_heads(
         (
             lax.all_to_all(head_groups(queries), "seq", split_axis=1, concat_axis=0, tiled=True),
             lax.all_to_all(head_groups(keys), "seq", split_axis=1, concat_axis=0, tiled=True),

time: 1140 us -> 604 us (0.53)
  local copies, waits for them, and re-layouts: 349 us -> 93.9 us
  matrix products: 258 us -> 14.8 us
  other arithmetic: 133 us -> 5.92 us
  waiting for transfers between devices: 262 us -> 342 us
  Pallas kernels: 0 us -> 76.6 us
  loops' own time: 59.5 us -> 0 us
    gather x60 -> x0, local copies, waits for them, and re-layouts: 250 us -> none  [the longest x20 75.4 us: grad_step(): chosen_keys = key_heads[picked]]
    dot_general x70 -> x0, matrix products: 242 us -> none  [the longest x10 59.6 us: output_step(): jnp.einsum('ihqk,ikhd->iqhd', prob_half, value_heads[picked], preferred_e...]
    scatter-add x20 -> x0, other arithmetic: 104 us -> none  [the longest x10 52 us: grad_step(): value_accum = value_accum.at[picked].add(value_terms)]
    all_gather x1, waiting for transfers between devices: 26.8 us -> 106 us  [on_device(): lax.all_gather(out_weight, 'fsdp', axis=0, tiled=True)]
    pallas_call x0 -> x1, Pallas kernels: none -> 76.6 us  [attend(): pl.pallas_call(attend_kernel, grid=(width // PAIR,), in_specs=[scalars, s...]
    another operation x3 -> x0, loops' own time: 59.5 us -> none  [the longest x1 20 us: head_forward(): lax.scan(stat_step, (start_max, start_sum), jnp.arange(MAXK))]
    reshape x4 -> x12, local copies, waits for them, and re-layouts: 9.88 us -> 39.9 us  [the longest x8 29.5 us: attend_heads(): member.reshape(-1, HEADS // seq_devices * HD)]
    reduce_sum x11 -> x0, other arithmetic: 19.9 us -> none  [the longest x10 15.8 us: stat_step(): row_sum = row_sum * jnp.exp(row_max - new_max) + jnp.sum(expo, axis=-1)]
  transfers between devices with their start and end apart: 10 -> 10, of which waited for: 8 -> 7; matrix products, arithmetic and copies ran while one was open for 61% -> 12% of each run, Pallas kernels for 0% -> 0%
where the time goes in v1:
time: 604 us; the launch traced here: 597 us
  waiting for transfers between devices  342 us (57%)
  local copies, waits for them, and re-layouts  93.9 us (16%)
  Pallas kernels  76.6 us (13%)
  starting transfers between devices  30.8 us (5%)
  blocking collectives  19.3 us (3%)
  matrix products  14.8 us (2%)
  between operations  14 us (2%)
    reduce_scatter x1, waiting for transfers between devices, on_device(): lax.psum_scatter(lax.dot_general(attn_out, loss_grad, (((0,), (0,)), ((),...  182 us
    all_gather x1, waiting for transfers between devices, on_device(): lax.all_gather(out_weight, 'fsdp', axis=0, tiled=True)  106 us
    pallas_call x1, Pallas kernels, attend(): pl.pallas_call(attend_kernel, grid=(width // PAIR,), in_specs=[scalars, s...  76.6 us
    unnamed x45, local copies, waits for them, and re-layouts  40.3 us
    reshape x8, local copies, waits for them, and re-layouts, attend_heads(): member.reshape(-1, HEADS // seq_devices * HD)  29.5 us
    all_to_all x1, blocking collectives, on_device(): lax.all_to_all(attn_heads, 'seq', split_axis=0, concat_axis=1, tiled=True)  19.3 us
    all_to_all x1, waiting for transfers between devices, on_device(): lax.all_to_all(head_groups(queries), 'seq', split_axis=1, concat_axis=0,...  14.1 us
    all_to_all x1, waiting for transfers between devices, on_device(): lax.all_to_all(head_groups(keys), 'seq', split_axis=1, concat_axis=0, til...  13.1 us
  transfers between devices with their start and end apart: 10, of which 7 were waited for; matrix products, arithmetic and copies ran while one was open for 12% of the time, Pallas kernels for 0%

profile of v1, /device:TPU:16, one launch (start us, length us, event | category | flops | bytes accessed | tf_op | source)
XLA Modules:
  0.0 597.3 jit_solution(13832295898949557238)
XLA Ops:
  14.8 14.1 %all-to-all-done = bf16[256,8,4,64]{0,3,2,1:T(8,128)(2,1)S(1)} async-done(((bf16[256,8,4,64]{0,3,2,1:T(8,128)(2,1)}), bf16[256,8,4,64]{0,3,2,1:T(8,128)(2,1)S(1)}, u32[]{:S(2)}, u32[]{:S(2)}) %all-to-all-start) | async-done | bytes 1048608 | tf_op jit(solution)/shard_map/all_to_all | solution.py:300
  34.8 13.1 %all-to-all-done.1 = bf16[256,8,4,64]{0,3,2,1:T(8,128)(2,1)S(1)} async-done(((bf16[256,8,4,64]{0,3,2,1:T(8,128)(2,1)}), bf16[256,8,4,64]{0,3,2,1:T(8,128)(2,1)S(1)}, u32[]{:S(2)}, u32[]{:S(2)}) %all-to-all-start.1) | async-done | bytes 1048608 | tf_op jit(solution)/shard_map/all_to_all | solution.py:301
  47.8 4.2 all-to-all-start.2
  52.1 106.5 %all-gather.3.cloned.1.call-done = bf16[2048,2048]{1,0:T(8,128)(2,1)} async-done(((bf16[512,2048]{1,0:T(8,128)(2,1)}), bf16[2048,2048]{1,0:T(8,128)(2,1)}) %all-gather.3.cloned.1.call-update) | async-done | bytes 8388624 | tf_op jit(solution)/shard_map/all_gather | solution.py:281
  158.6 6.7 %convolution_convert_fusion = bf16[256,2048]{1,0:T(8,128)(2,1)} fusion(bf16[2048,2048]{1,0:T(8,128)(2,1)} %all-gather.3.cloned.1.call-done, bf16[1,256,2048]{2,1,0:T(8,128)(2,1)S(1)} %copy-done), kind=kOutput, calls=%fused_computation | convolution fusion | flops 2148007936 | bytes 10485760 | tf_op jit(solution)/shard_map/dot_general | solution.py:279
  167.6 4.2 all-to-all-start.3
  180.4 4.3 reshape.65.key
  188.8 4.3 reshape.66.value
  197.1 4.3 reshape.67.grad
  201.4 76.6 %attend.1 = (bf16[2048,256]{1,0:T(8,128)(2,1)S(1)}, bf16[2048,256]{1,0:T(8,128)(2,1)S(1)}, bf16[2048,256]{1,0:T(8,128)(2,1)S(1)}, bf16[2048,256]{1,0:T(8,128)(2,1)S(1)}) custom-call(s32[16,10]{1,0:T(8,128)S(1)} %bitcast.57, s32[16]{0:T(128)S(1)} %bitcast.58, bf16[2048,256]{1,0:T(8,128)(2,1)S(1)} %reshape.64.query, bf16[2048,256]{1,0:T(8,128)(2,1)} %reshape.65.key, ...), custom_call_target="tpu_custom_call" | custom-call | flops 8053063680 | bytes 8388608 | tf_op jit(solution)/shard_map/attend/pallas_call | solution.py:243
  288.3 19.3 %all_to_all.120 = bf16[8,2,32768]{2,1,0:T(2,128)(2,1)} all-to-all(bf16[8,2,32768]{2,1,0:T(2,128)(2,1)S(1)} %reshape.74), channel_id=1, replica_groups=mesh['fsdp'=4,'seq'=8] {'seq'}, dimensions={0} | all-to-all | bytes 2097152 | tf_op jit(solution)/shard_map/all_to_all | solution.py:312
  307.6 4.3 reshape.75
  314.7 8.1 %fusion = f32[2048,2048]{1,0:T(8,128)} fusion(bf16[256,2048]{0,1:T(8,128)(2,1)S(1)} %bitcast.63, bf16[1,256,2048]{2,1,0:T(8,128)(2,1)S(1)} %copy-done), kind=kOutput, calls=%fused_computation.1 | convolution fusion | flops 2147483648 | bytes 18874368 | tf_op jit(solution)/shard_map/dot_general | solution.py:316
  322.9 181.6 %reduce-scatter.2.cloned.1.call-done = f32[64,2048]{1,0:T(8,128)} async-done(((f32[2048,2048]{1,0:T(8,128)}), f32[64,2048]{1,0:T(8,128)}) %reduce-scatter.2.cloned.1.call-update) | async-done | bytes 524304 | tf_op jit(solution)/shard_map/reduce_scatter | solution.py:315
  509.6 4.4 reshape.68
  514.1 6.4 %all-to-all-start.4 = ((bf16[8,2,32768]{2,1,0:T(2,128)(2,1)}), bf16[8,2,32768]{2,1,0:T(2,128)(2,1)S(1)}, u32[]{:S(2)}, u32[]{:S(2)}) async-start(bf16[8,2,32768]{2,1,0:T(2,128)(2,1)} %reshape.68), calls=%async_computation.4 | async-start | bytes 2097152 | tf_op jit(solution)/shard_map/all_to_all | solution.py:309
  521.9 4.0 copy.85
  526.0 4.3 reshape.70
  530.3 9.4 %all-to-all-done.4 = bf16[8,2,32768]{2,1,0:T(2,128)(2,1)S(1)} async-done(((bf16[8,2,32768]{2,1,0:T(2,128)(2,1)}), bf16[8,2,32768]{2,1,0:T(2,128)(2,1)S(1)}, u32[]{:S(2)}, u32[]{:S(2)}) %all-to-all-start.4) | async-done | bytes 1048608 | tf_op jit(solution)/shard_map/all_to_all | solution.py:309
  539.7 4.3 all-to-all-start.5
  548.7 10.7 %all-to-all-done.5 = bf16[8,2,32768]{2,1,0:T(2,128)(2,1)} async-done(((bf16[8,2,32768]{2,1,0:T(2,128)(2,1)}), bf16[8,2,32768]{2,1,0:T(2,128)(2,1)}, u32[]{:S(2)}, u32[]{:S(2)}) %all-to-all-start.5) | async-done | bytes 1048608 | tf_op jit(solution)/shard_map/all_to_all | solution.py:310
  559.3 4.2 all-to-all-start.6
  573.1 5.9 all-to-all-done.6
  586.7 4.1 convert_element_type.11
  (71 shorter events, 73.8 us)
Async XLA Ops:
  7.2 151.4 %copy-start = (bf16[1,256,2048]{2,1,0:T(8,128)(2,1)S(1)}, bf16[1,256,2048]{2,1,0:T(8,128)(2,1)}, u32[]{:S(2)}) copy-start(bf16[1,256,2048]{2,1,0:T(8,128)(2,1)} %param.10) | copy-start | bytes 3145732
  7.2 1.3 copy-start.12
  7.2 151.4 %all-gather.3.cloned.1.call-start = ((), (), s32[]{:S(2)}) async-start(), calls=%async_computation.9 | async-start | bytes 10485760 | tf_op jit(solution)/shard_map/all_gather | solution.py:281
  8.5 5.0 copy-start.13
  9.8 19.1 %all-to-all-start = ((bf16[256,8,4,64]{0,3,2,1:T(8,128)(2,1)}), bf16[256,8,4,64]{0,3,2,1:T(8,128)(2,1)S(1)}, u32[]{:S(2)}, u32[]{:S(2)}) async-start(bf16[256,8,4,64]{0,3,2,1:T(8,128)(2,1)} %bitcast.2), calls=%async_computation | async-start | bytes 2097152 | tf_op jit(solution)/shard_map/all_to_all | solution.py:300
  28.9 18.9 %all-to-all-start.1 = ((bf16[256,8,4,64]{0,3,2,1:T(8,128)(2,1)}), bf16[256,8,4,64]{0,3,2,1:T(8,128)(2,1)S(1)}, u32[]{:S(2)}, u32[]{:S(2)}) async-start(bf16[256,8,4,64]{0,3,2,1:T(8,128)(2,1)} %bitcast.75), calls=%async_computation.1 | async-start | bytes 2097152 | tf_op jit(solution)/shard_map/all_to_all | solution.py:301
  47.8 117.5 %copy-start.8 = (bf16[256,8,4,64]{0,3,2,1:T(8,128)(2,1)}, bf16[256,8,4,64]{0,3,2,1:T(8,128)(2,1)S(1)}, u32[]{:S(2)}) copy-start(bf16[256,8,4,64]{0,3,2,1:T(8,128)(2,1)S(1)} %all-to-all-done.1) | copy-start | bytes 3145732
  47.8 119.7 %all-to-all-start.2 = ((bf16[256,8,4,64]{0,3,2,1:T(8,128)(2,1)}), bf16[256,8,4,64]{0,3,2,1:T(8,128)(2,1)}, u32[]{:S(2)}, u32[]{:S(2)}) async-start(bf16[256,8,4,64]{0,3,2,1:T(8,128)(2,1)} %bitcast.74), calls=%async_computation.2 | async-start | bytes 2097152 | tf_op jit(solution)/shard_map/all_to_all | solution.py:302
  165.3 6.6 %copy-start.14 = (s32[1,16,10]{1,0,2:T(1,128)S(1)}, s32[1,16,10]{1,0,2:T(1,128)}, u32[]{:S(2)}) copy-start(s32[1,16,10]{1,0,2:T(1,128)} %param.12) | copy-start | bytes 1924
  167.6 25.5 %all-to-all-start.3 = ((bf16[256,8,4,64]{0,3,2,1:T(8,128)(2,1)}), bf16[256,8,4,64]{0,3,2,1:T(8,128)(2,1)}, u32[]{:S(2)}, u32[]{:S(2)}) async-start(bf16[256,8,4,64]{0,3,2,1:T(8,128)(2,1)} %bitcast.73), calls=%async_computation.3 | async-start | bytes 2097152 | tf_op jit(solution)/shard_map/all_to_all | solution.py:303
  171.8 332.6 %reduce-scatter.2.cloned.1.call-start = ((), (), s32[]{:S(2)}) async-start(), calls=%async_computation.10 | async-start | bytes 17301504 | tf_op jit(solution)/shard_map/reduce_scatter | solution.py:315
  174.4 3.6 copy-start.9
  197.1 4.3 copy-start.7
  278.0 1.0 copy-start.2
  279.0 1.0 copy-start.4
  322.8 183.5 %copy-start.5 = (bf16[2048,256]{1,0:T(8,128)(2,1)S(1)}, bf16[2048,256]{1,0:T(8,128)(2,1)}, u32[]{:S(2)}) copy-start(bf16[2048,256]{1,0:T(8,128)(2,1)} %copy-done.4) | copy-start | bytes 3145732
  322.8 263.8 %all-gather.5.cloned.1.call-start = ((), (), s32[]{:S(2)}) async-start(), calls=%async_computation.11 | async-start | bytes 2359296 | tf_op jit(solution)/shard_map/all_gather | solution.py:323
  509.6 10.8 %copy-start.3 = (bf16[2048,256]{1,0:T(8,128)(2,1)S(1)}, bf16[2048,256]{1,0:T(8,128)(2,1)}, u32[]{:S(2)}) copy-start(bf16[2048,256]{1,0:T(8,128)(2,1)} %copy-done.2) | copy-start | bytes 3145732
  514.1 25.6 %all-to-all-start.4 = ((bf16[8,2,32768]{2,1,0:T(2,128)(2,1)}), bf16[8,2,32768]{2,1,0:T(2,128)(2,1)S(1)}, u32[]{:S(2)}, u32[]{:S(2)}) async-start(bf16[8,2,32768]{2,1,0:T(2,128)(2,1)} %reshape.68), calls=%async_computation.4 | async-start | bytes 2097152 | tf_op jit(solution)/shard_map/all_to_all | solution.py:309
  539.7 4.9 copy-start.10
  539.7 19.7 %all-to-all-start.5 = ((bf16[8,2,32768]{2,1,0:T(2,128)(2,1)}), bf16[8,2,32768]{2,1,0:T(2,128)(2,1)}, u32[]{:S(2)}, u32[]{:S(2)}) async-start(bf16[8,2,32768]{2,1,0:T(2,128)(2,1)} %reshape.70), calls=%async_computation.5 | async-start | bytes 2097152 | tf_op jit(solution)/shard_map/all_to_all | solution.py:310
  546.0 17.6 %copy-start.11 = (bf16[8,2,32768]{2,1,0:T(2,128)(2,1)S(1)}, bf16[8,2,32768]{2,1,0:T(2,128)(2,1)}, u32[]{:S(2)}) copy-start(bf16[8,2,32768]{2,1,0:T(2,128)(2,1)} %copy-done.10) | copy-start | bytes 3145732
  559.3 19.7 %all-to-all-start.6 = ((bf16[8,2,32768]{2,1,0:T(2,128)(2,1)}), bf16[8,2,32768]{2,1,0:T(2,128)(2,1)}, u32[]{:S(2)}, u32[]{:S(2)}) async-start(bf16[8,2,32768]{2,1,0:T(2,128)(2,1)} %reshape.72), calls=%async_computation.6 | async-start | bytes 2097152 | tf_op jit(solution)/shard_map/all_to_all | solution.py:311
  584.3 6.5 %copy-start.1 = (bf16[1,256,2048]{2,1,0:T(8,128)(2,1)S(1)}, bf16[1,256,2048]{2,1,0:T(8,128)(2,1)}, u32[]{:S(2)}) copy-start(bf16[1,256,2048]{2,1,0:T(8,128)(2,1)} %param.10) | copy-start | bytes 3145732
  (1 other events, 1.0 us)
Sparse Core Ops, SparseCore 0:
  9.6 148.9 all-gather.2
  323.0 181.4 reduce-scatter.1
  506.4 35.7 all-gather.4

commit v2 on v0

--- a/solution.py
+++ b/solution.py
@@ -1,6 +1,11 @@
+import functools
+import math
+
 import jax
 import jax.numpy as jnp
 from jax import lax
+from jax.experimental import pallas as pl
+from jax.experimental.pallas import tpu as pltpu
 from jax.sharding import PartitionSpec as P
 
 HEADS = 32
@@ -118,7 +123,412 @@
     )
 
 
-def on_device(queries, keys, values, out_grad, out_weight, key_blocks, block_counts):
+PAIR = 2 * HD
+PAIR = 2 * HD
+SCALE = HD ** (-0.5)
+BASE2 = SCALE * math.log2(math.e)
+
+
+def fold_rows(tile, combine):
+    return combine(tile.reshape(-1, 8, tile.shape[1]), axis=0)
+
+
+def block_rows(index, height=BLK):
+    return pl.ds(pl.multiple_of(index * height, height), height)
+
+
+def by_head(block):
+    first = lax.broadcasted_iota(jnp.int32, block.shape, 1) < HD
+    zero = jnp.zeros_like(block)
+    return jnp.concatenate([jnp.where(first, block, zero), jnp.where(first, zero, block)], axis=0)
+
+
+def by_head_t(block):
+    turned = block.T
+    first = lax.broadcasted_iota(jnp.int32, turned.shape, 0) < HD
+    zero = jnp.zeros_like(turned)
+    return jnp.concatenate([jnp.where(first, turned, zero), jnp.where(first, zero, turned)], axis=1)
+
+
+def own_parts(wide):
+    return jnp.concatenate([wide[:HD, :BLK], wide[HD:, BLK:]], axis=0)
+
+
+def dot(left, right):
+    return lax.dot_general(left, right, (((1,), (0,)), ((), ())), preferred_element_type=jnp.float32)
+
+
+def each_block(counts, blocks, body):
+    @pl.loop(0, blocks)
+    def _(index):
+        for slots in range(2, MAXK + 1, 2):
+            @pl.when((counts[index] + 1) // 2 == slots // 2)
+            def _():
+                body(index, slots)
+
+
+def forward_kernel(adjacency, counts, packed, attn_out, stats, value_t, raw, *, blocks):
+    query, key, value = (packed.at[:, pl.ds(PAIR * part, PAIR)] for part in range(3))
+
+    @pl.loop(0, blocks)
+    def _(index):
+        value_t[index] = value[block_rows(index), :].T
+
+    def query_block(index, slots):
+        live = counts[index]
+        picked = [adjacency[index, slot] for slot in range(slots)]
+        queries = by_head_t(query[block_rows(index), :])
+        row_max = jnp.full((8, 2 * BLK), NEG_FILL, jnp.float32)
+        for slot in range(slots):
+            score = dot(key[block_rows(picked[slot]), :], queries)
+            if slot == slots - 1:
+                score = jnp.where(slot < live, score, NEG_FILL)
+            raw[slot] = score
+            row_max = jnp.maximum(row_max, fold_rows(score, jnp.max))
+        row_max = jnp.max(row_max, axis=0, keepdims=True)
+        row_sum = jnp.zeros((8, 2 * BLK), jnp.float32)
+        out_t = jnp.zeros((PAIR, 2 * BLK), jnp.float32)
+        for slot in range(0, slots, 2):
+            halves = []
+            for each in (slot, slot + 1):
+                expo = jnp.exp2((raw[each] - row_max) * BASE2)
+                row_sum = row_sum + fold_rows(expo, jnp.sum)
+                halves.append(expo.astype(jnp.bfloat16))
+            out_t = out_t + dot(
+                jnp.concatenate([value_t[picked[slot]], value_t[picked[slot + 1]]], axis=1),
+                jnp.concatenate(halves, axis=0),
+            )
+        row_sum = jnp.sum(row_sum, axis=0, keepdims=True)
+        out_t = own_parts(out_t / row_sum)
+        attn_out[block_rows(index), :] = out_t.T.astype(jnp.bfloat16)
+        stats[block_rows(index, 8), :] = jnp.broadcast_to(
+            row_max * BASE2 + jnp.log2(row_sum), (8, 2 * BLK)
+        )
+
+    each_block(counts, blocks, query_block)
+
+
+def backward_kernel(
+    adjacency, counts, packed, grad, attn_out, stats, packed_g, key_t, key_sum, value_sum, *, blocks
+):
+    query, key, value = (packed.at[:, pl.ds(PAIR * part, PAIR)] for part in range(3))
+
+    @pl.loop(0, blocks)
+    def _(index):
+        key_t[index] = key[block_rows(index), :].T
+        key_sum[block_rows(index), :] = jnp.zeros((BLK, PAIR), jnp.float32)
+        value_sum[block_rows(index), :] = jnp.zeros((BLK, PAIR), jnp.float32)
+
+    def query_block(index, slots):
+        live = counts[index]
+        picked = [adjacency[index, slot] for slot in range(slots)]
+        query_rows = query[block_rows(index), :]
+        grad_rows = grad[block_rows(index), :]
+        queries, queries_t = by_head(query_rows), by_head_t(query_rows)
+        grads, grads_t = by_head(grad_rows), by_head_t(grad_rows)
+        stat = stats[pl.ds(pl.multiple_of(index * 8, 8), 1), :]
+        products = (
+            grad_rows.astype(jnp.float32) * attn_out[block_rows(index), :].astype(jnp.float32)
+        ).T
+        row_dot = jnp.concatenate(
+            [
+                jnp.sum(products[:HD], axis=0, keepdims=True),
+                jnp.sum(products[HD:], axis=0, keepdims=True),
+            ],
+            axis=1,
+        )
+        query_t = jnp.zeros((PAIR, 2 * BLK), jnp.float32)
+        for slot in range(0, slots, 2):
+            terms = []
+            for each in (slot, slot + 1):
+                at = block_rows(picked[each])
+                prob = jnp.exp2(dot(key[at, :], queries_t) * BASE2 - stat)
+                if each == slots - 1:
+                    prob = jnp.where(each < live, prob, 0.0)
+                prob_grad = dot(value[at, :], grads_t)
+                term = (prob * (prob_grad - row_dot)).astype(jnp.bfloat16)
+                key_sum[at, :] += dot(term, queries)
+                value_sum[at, :] += dot(prob.astype(jnp.bfloat16), grads)
+                terms.append(term)
+            query_t = query_t + dot(
+                jnp.concatenate([key_t[picked[slot]], key_t[picked[slot + 1]]], axis=1),
+                jnp.concatenate(terms, axis=0),
+            )
+        packed_g[block_rows(index), :PAIR] = (own_parts(query_t).T * SCALE).astype(jnp.bfloat16)
+
+    each_block(counts, blocks, query_block)
+    packed_g[:, PAIR : 2 * PAIR] = (key_sum[...] * SCALE).astype(jnp.bfloat16)
+    packed_g[:, 2 * PAIR :] = value_sum[...].astype(jnp.bfloat16)
+
+
+VMEM = pl.BlockSpec(memory_space=pltpu.VMEM)
+SMEM = pl.BlockSpec(memory_space=pltpu.SMEM)
+PARAMS = pltpu.CompilerParams(vmem_limit_bytes=48 * 2**20)
+
+
+def cost(tokens, products):
+    tiles = tokens // BLK * MAXK * 2
+    return pl.CostEstimate(
+        flops=tiles * products * 2 * BLK * BLK * HD * 16,
+        bytes_accessed=12 * tokens * PAIR,
+        transcendentals=tiles * BLK * BLK,
+    )
+
+
+def forward(packed, adjacency, counts):
+    tokens = packed.shape[0]
+    blocks = tokens // BLK
+    return pl.pallas_call(
+        functools.partial(forward_kernel, blocks=blocks),
+        in_specs=[SMEM, SMEM, VMEM],
+        out_specs=[VMEM, VMEM],
+        out_shape=[
+            jax.ShapeDtypeStruct((tokens, PAIR), jnp.bfloat16),
+            jax.ShapeDtypeStruct((blocks * 8, 2 * BLK), jnp.float32),
+        ],
+        scratch_shapes=[
+            pltpu.VMEM((blocks, PAIR, BLK), jnp.bfloat16),
+            pltpu.VMEM((MAXK, BLK, 2 * BLK), jnp.float32),
+        ],
+        compiler_params=PARAMS,
+        cost_estimate=cost(tokens, 2),
+        name="attend_forward",
+    )(adjacency, counts, packed)
+
+
+def backward(packed, grad, pair, attn_out, stats, adjacency, counts):
+    tokens = packed.shape[0]
+    blocks = tokens // BLK
+    whole = lambda array: pl.BlockSpec(array.shape, lambda step: (0, 0))
+    return pl.pallas_call(
+        functools.partial(backward_kernel, blocks=blocks),
+        grid=(1,),
+        in_specs=[
+            SMEM, SMEM, whole(packed), pl.BlockSpec((tokens, PAIR), lambda step: (0, pair)),
+            whole(attn_out), whole(stats),
+        ],
+        out_specs=whole(packed),
+        out_shape=jax.ShapeDtypeStruct(packed.shape, jnp.bfloat16),
+        scratch_shapes=[
+            pltpu.VMEM((blocks, PAIR, BLK), jnp.bfloat16),
+            pltpu.VMEM((tokens, PAIR), jnp.float32),
+            pltpu.VMEM((tokens, PAIR), jnp.float32),
+        ],
+        compiler_params=PARAMS,
+        cost_estimate=cost(tokens, 5),
+        name="attend_backward",
+    )(adjacency, counts, packed, grad, attn_out, stats)
+
+
+def pack_kernel(queries, keys, values, first, second):
+    for group in range(first.shape[0]):
+        for pair, out in enumerate((first, second)):
+            start = PAIR * (2 * group + pair)
+            for part, source in enumerate((queries, keys, values)):
+                out[group, :, PAIR * part : PAIR * (part + 1)] = source[:, start : start + PAIR]
+
+
+def pack(queries, keys, values, groups):
+    tokens, width = queries.shape
+    height = tokens // 4
+    taken = pl.BlockSpec((height, width), lambda step: (step, 0))
+    given = pl.BlockSpec((groups, height, 3 * PAIR), lambda step: (0, step, 0))
+    return pl.pallas_call(
+        pack_kernel,
+        grid=(4,),
+        in_specs=[taken] * 3,
+        out_specs=[given] * 2,
+        out_shape=[jax.ShapeDtypeStruct((groups, tokens, 3 * PAIR), queries.dtype)] * 2,
+        compiler_params=PARAMS,
+        name="pack",
+    )(queries, keys, values)
+
+
+def unpack_kernel(first, second, query_g, key_g, value_g):
+    for group in range(first.shape[0]):
+        for pair, source in enumerate((first, second)):
+            start = PAIR * (2 * group + pair)
+            for part, out in enumerate((query_g, key_g, value_g)):
+                out[:, start : start + PAIR] = source[group, :, PAIR * part : PAIR * (part + 1)]
+
+
+def unpack(first, second):
+    groups, tokens, _ = first.shape
+    height = tokens // 4
+    taken = pl.BlockSpec((groups, height, 3 * PAIR), lambda step: (0, step, 0))
+    given = pl.BlockSpec((height, groups * 2 * PAIR), lambda step: (step, 0))
+    return pl.pallas_call(
+        unpack_kernel,
+        grid=(4,),
+        in_specs=[taken] * 2,
+        out_specs=[given] * 3,
+        out_shape=[jax.ShapeDtypeStruct((tokens, groups * 2 * PAIR), first.dtype)] * 3,
+        compiler_params=PARAMS,
+        name="unpack",
+    )(first, second)
+
+
+def spread_kernel(gathered, out):
+    groups, _, width = gathered.shape
+    for group in range(groups):
+        out[:, width * group : width * (group + 1)] = gathered[group].astype(out.dtype)
+
+
+def spread(gathered):
+    groups, rows, columns = gathered.shape
+    height = rows // 8
+    return pl.pallas_call(
+        spread_kernel,
+        grid=(8,),
+        in_specs=[pl.BlockSpec((groups, height, columns), lambda step: (0, step, 0))],
+        out_specs=pl.BlockSpec((height, groups * columns), lambda step: (step, 0)),
+        out_shape=jax.ShapeDtypeStruct((rows, groups * columns), jnp.float32),
+        compiler_params=PARAMS,
+        name="spread",
+    )(gathered)
+
+
+def exchange(chunks):
+    return lax.all_to_all(chunks, "seq", split_axis=0, concat_axis=0, tiled=True)
+
+
+def weight_rows_sent(out_weight, member, planes, members):
+    per_plane = members // planes
+    height = out_weight.shape[0] // per_plane
+    own = lax.dynamic_slice_in_dim(out_weight, (member % per_plane) * height, height)
+    received = [own]
+    for offset in range(1, planes):
+        routes = [
+            (s // per_plane * members + s, (s // per_plane ^ offset) * members + s)
+            for s in range(members)
+        ]
+        received.append(lax.ppermute(own, ("fsdp", "seq"), routes))
+    return received
+
+
+def gather_pieces(shard, members):
+    def swap(array, mask):
+        return lax.ppermute(array, "seq", [(s, s ^ mask) for s in range(members)])
+
+    height = shard.shape[0] // 2
+    along, across = swap(shard, 2), swap(shard, 4)
+    pieces = [
+        (0, 0, shard),
+        (2, 0, along),
+        (4, 0, across),
+        (6, 0, swap(along[:height], 4)),
+        (6, height, swap(across[height:], 2)),
+    ]
+    return pieces + [(mask ^ 1, row, swap(piece, 1)) for mask, row, piece in pieces]
+
+
+def project_kernel(places, where, *refs, offsets, groups):
+    count = len(places)
+    pieces, rest = refs[:count], refs[count:]
+    weights, (first, second, attn_grad, terms, whole, weight, landed, fetched) = rest[:offsets], rest[offsets:]
+    local = whole.shape[0] // groups
+    copies = []
+    for number, (mask, row) in enumerate(places):
+        start = pl.multiple_of((where[0] ^ mask) * local + row, BLK)
+        target = whole.at[pl.ds(start, pieces[number].shape[0]), :]
+        copies.append((start, pltpu.make_async_copy(pieces[number], target, landed.at[number])))
+    for offset in range(offsets):
+        @pl.when(where[1] == offset)
+        def _():
+            pltpu.make_async_copy(weights[offset], weight, fetched).start()
+    for _, copy in copies:
+        copy.start()
+    pltpu.make_async_copy(weights[0], weight, fetched).wait()
+    for number, (start, copy) in enumerate(copies):
+        copy.wait()
+        rows = pl.ds(start, pieces[number].shape[0])
+        attn_grad[rows, :] = lax.dot_general(
+            whole[rows, :], weight[...], (((1,), (1,)), ((), ())), preferred_element_type=jnp.float32
+        ).astype(jnp.bfloat16)
+    width = whole.shape[1] // groups
+    attn_t = jnp.concatenate([first[...].T, second[...].T], axis=0)
+    for group in range(groups):
+        terms[group] = dot(attn_t, whole[:, width * group : width * (group + 1)]).astype(jnp.bfloat16)
+
+
+def project(pieces, weights, first, second, where, groups):
+    places = [(mask, row) for mask, row, _ in pieces]
+    arrays = [piece for _, _, piece in pieces]
+    height, width = weights[0].shape
+    tokens = first.shape[0]
+    far = pl.BlockSpec(memory_space=pl.ANY)
+    return pl.pallas_call(
+        lambda *refs: project_kernel(places, *refs, offsets=len(weights), groups=groups),
+        in_specs=[SMEM] + [far] * (len(arrays) + len(weights)) + [VMEM] * 2,
+        out_specs=[VMEM] * 2,
+        out_shape=[
+            jax.ShapeDtypeStruct((tokens, height), jnp.bfloat16),
+            jax.ShapeDtypeStruct((groups, height, width // groups), jnp.bfloat16),
+        ],
+        scratch_shapes=[
+            pltpu.VMEM((tokens, width), jnp.bfloat16),
+            pltpu.VMEM((height, width), jnp.bfloat16),
+            pltpu.SemaphoreType.DMA((len(arrays),)),
+            pltpu.SemaphoreType.DMA,
+        ],
+        compiler_params=PARAMS,
+        cost_estimate=pl.CostEstimate(
+            flops=4 * tokens * width * height,
+            bytes_accessed=2 * tokens * width + 8 * height * width,
+            transcendentals=0,
+        ),
+        name="project",
+    )(where, *arrays, *weights, first, second)
+
+
+def plane_sum(rows, plane, planes):
+    height = rows.shape[0] // planes
+
+    def part(offset):
+        return lax.dynamic_slice_in_dim(rows, (plane ^ offset) * height, height)
+
+    total = part(0).astype(jnp.float32)
+    for offset in range(1, planes):
+        routes = [(z, z ^ offset) for z in range(planes)]
+        total = total + lax.ppermute(part(offset), "fsdp", routes).astype(jnp.float32)
+    return total
+
+
+def fits_pairs(sizes):
+    planes, members = sizes["fsdp"], sizes["seq"]
+    return members == 8 and planes == 4 and members * 2 * PAIR == HEADS * HD
+
+
+def pair_device(queries, keys, values, out_grad, out_weight, key_blocks, block_counts):
+    planes, members = lax.axis_size("fsdp"), lax.axis_size("seq")
+    plane, member = lax.axis_index("fsdp"), lax.axis_index("seq")
+    local_tokens, model_width = queries.shape[1:]
+    tokens = local_tokens * members
+    adjacency, counts = key_blocks[0], block_counts[0]
+
+    chunks = pack(queries[0], keys[0], values[0], members)
+    packed = [exchange(chunk).reshape(tokens, 3 * PAIR) for chunk in chunks]
+    weights = weight_rows_sent(out_weight, member, planes, members)
+    pieces = gather_pieces(out_grad[0], members)
+    forwards = [forward(one, adjacency, counts) for one in packed]
+    where = jnp.stack([member, plane ^ (member // (members // planes))]).astype(jnp.int32)
+    attn_grad, by_columns = project(
+        pieces, weights, forwards[0][0], forwards[1][0], where, members
+    )
+    returned = []
+    for pair in range(2):
+        attn_out, stats = forwards[pair]
+        packed_g = backward(packed[pair], attn_grad, pair, attn_out, stats, adjacency, counts)
+        returned.append(exchange(packed_g.reshape(members, local_tokens, 3 * PAIR)))
+    query_g, key_g, value_g = unpack(*returned)
+
+    columns = exchange(by_columns).reshape(model_width, -1)
+    summed = plane_sum(columns, plane, planes).astype(jnp.bfloat16)
+    wo_grad = spread(lax.all_gather(summed, "seq", axis=0))
+    return (query_g[None], key_g[None], value_g[None], wo_grad)
+
+
+def general_device(queries, keys, values, out_grad, out_weight, key_blocks, block_counts):
     local_tokens = queries.shape[1]
     model_width = queries.shape[2]
     seq_devices = lax.axis_size("seq")
@@ -179,9 +589,13 @@
     return (to_tokens(query_t), to_tokens(key_t), to_tokens(value_t), wo_grad)
 
 
+def on_device(mesh):
+    return pair_device if fits_pairs(mesh.shape) else general_device
+
+
 def solution(mesh):
     return jax.shard_map(
-        on_device,
+        on_device(mesh),
         mesh=mesh,
         in_specs=(
             P("fsdp", "seq", None),

time: 1140 us -> 269 us (0.24)
  the two profiles are of different devices: /device:TPU:16 before, /device:TPU:24 now
where the time goes in v2:
time: 269 us; the launch traced here: 267 us
  Pallas kernels  118 us (44%)
  waiting for transfers between devices  55.7 us (21%)
  starting transfers between devices  33.4 us (12%)
  blocking collectives  25 us (9%)
  local copies, waits for them, and re-layouts  18.7 us (7%)
  between operations  14.3 us (5%)
    pallas_call x2, Pallas kernels, backward(): pl.pallas_call(functools.partial(backward_kernel, blocks=blocks), grid=(1...  63.5 us
    ppermute x9, waiting for transfers between devices, swap(): return lax.ppermute(array, 'seq', [(s, s ^ mask) for s in range(members)])  33.4 us
    pallas_call x2, Pallas kernels, forward(): pl.pallas_call(functools.partial(forward_kernel, blocks=blocks), in_specs...  32.1 us
    all_to_all x1, blocking collectives, exchange(): lax.all_to_all(chunks, 'seq', split_axis=0, concat_axis=0, tiled=True)  25 us
    all_to_all x4, waiting for transfers between devices, exchange(): lax.all_to_all(chunks, 'seq', split_axis=0, concat_axis=0, tiled=True)  22.3 us
    all_to_all x4, starting transfers between devices, exchange(): lax.all_to_all(chunks, 'seq', split_axis=0, concat_axis=0, tiled=True)  17.6 us
    pallas_call x1, Pallas kernels, project(): pl.pallas_call(lambda *refs: project_kernel(places, *refs, offsets=len(we...  12.5 us
    unnamed x35, local copies, waits for them, and re-layouts  11.8 us
  transfers between devices with their start and end apart: 20, of which 3 were waited for; matrix products, arithmetic and copies ran while one was open for 3% of the time, Pallas kernels for 37%

profile of v2, /device:TPU:24, one launch (start us, length us, event | category | flops | bytes accessed | tf_op | source)
XLA Modules:
  0.0 267.2 jit_solution(12177646973876662529)
XLA Ops:
  11.0 2.0 pack.1
  14.2 4.3 %all-to-all-start = ((bf16[8,256,384]{2,1,0:T(8,128)(2,1)}), bf16[8,256,384]{2,1,0:T(8,128)(2,1)}, u32[]{:S(2)}, u32[]{:S(2)}) async-start(bf16[8,256,384]{2,1,0:T(8,128)(2,1)} %copy-done.2), calls=%async_computation | async-start | bytes 3145728 | tf_op jit(solution)/shard_map/all_to_all | solution.py:392
  18.5 1.9 collective-permute-start
  23.0 1.7 collective-permute-start.10
  26.0 1.7 collective-permute-start.9
  27.8 33.3 %collective-permute-done.refs_2_ = bf16[256,2048]{1,0:T(8,128)(2,1)} collective-permute-done((bf16[256,2048]{1,0:T(8,128)(2,1)}, bf16[256,2048]{1,0:T(8,128)(2,1)}, u32[]{:S(2)}, u32[]{:S(2)}) %collective-permute-start) | collective-permute-done | bytes 1048608 | tf_op jit(solution)/shard_map/ppermute | solution.py:411
  61.1 1.9 slice.8
  64.5 1.9 slice.9
  66.9 4.4 %all-to-all-start.1 = ((bf16[8,256,384]{2,1,0:T(8,128)(2,1)}), bf16[8,256,384]{2,1,0:T(8,128)(2,1)}, u32[]{:S(2)}, u32[]{:S(2)}) async-start(bf16[8,256,384]{2,1,0:T(8,128)(2,1)} %get-tuple-element.17), calls=%async_computation.1 | async-start | bytes 3145728 | tf_op jit(solution)/shard_map/all_to_all | solution.py:392
  71.4 16.0 %attend_forward.2 = (bf16[2048,128]{1,0:T(8,128)(2,1)S(1)}, f32[128,256]{1,0:T(8,128)S(1)}) custom-call(s32[16,10]{1,0:T(8,128)S(1)} %bitcast.23, s32[16]{0:T(128)S(1)} %bitcast.27, bf16[2048,384]{1,0:T(8,128)(2,1)} %bitcast.5.packed), custom_call_target="tpu_custom_call" | custom-call | flops 21474836480 | bytes 3145728 | tf_op jit(solution)/shard_map/attend_forward/pallas_call | solution.py:281
  89.7 7.1 %all-to-all-done.1 = bf16[8,256,384]{2,1,0:T(8,128)(2,1)} async-done(((bf16[8,256,384]{2,1,0:T(8,128)(2,1)}), bf16[8,256,384]{2,1,0:T(8,128)(2,1)}, u32[]{:S(2)}, u32[]{:S(2)}) %all-to-all-start.1) | async-done | bytes 1572896 | tf_op jit(solution)/shard_map/all_to_all | solution.py:392
  96.7 16.1 %attend_forward.3 = (bf16[2048,128]{1,0:T(8,128)(2,1)S(1)}, f32[128,256]{1,0:T(8,128)S(1)}) custom-call(s32[16,10]{1,0:T(8,128)S(1)} %bitcast.24, s32[16]{0:T(128)S(1)} %bitcast.28, bf16[2048,384]{1,0:T(8,128)(2,1)} %bitcast.9.packed), custom_call_target="tpu_custom_call" | custom-call | flops 21474836480 | bytes 3145728 | tf_op jit(solution)/shard_map/attend_forward/pallas_call | solution.py:281
  112.9 12.5 %project.1 = (bf16[2048,256]{1,0:T(8,128)(2,1)S(1)}, bf16[8,256,256]{2,1,0:T(8,128)(2,1)}) custom-call(s32[2]{0:T(128)S(1)} %pad_add_fusion.refs_0_, bf16[256,2048]{1,0:T(8,128)(2,1)} %bitcast.8.refs_1_, bf16[256,2048]{1,0:T(8,128)(2,1)} %collective-permute-done.refs_2_, bf16[256,2048]{1,0:T(8,128)(2,1)} %collective-permute-done.1.refs_3_, ...), custom_call_target="tpu_custom_call" | custom-call | flops 4294967296 | bytes 12582912 | tf_op jit(solution)/shard_map/project/pallas_call | solution.py:460
  126.4 4.6 %all-to-all-start.4 = ((bf16[8,256,256]{2,1,0:T(8,128)(2,1)}), bf16[8,256,256]{2,1,0:T(8,128)(2,1)}, u32[]{:S(2)}, u32[]{:S(2)}) async-start(bf16[8,256,256]{2,1,0:T(8,128)(2,1)} %get-tuple-element.25), calls=%async_computation.4 | async-start | bytes 2097152 | tf_op jit(solution)/shard_map/all_to_all | solution.py:392
  131.0 15.2 %all-to-all-done.4 = bf16[8,256,256]{2,1,0:T(8,128)(2,1)} async-done(((bf16[8,256,256]{2,1,0:T(8,128)(2,1)}), bf16[8,256,256]{2,1,0:T(8,128)(2,1)}, u32[]{:S(2)}, u32[]{:S(2)}) %all-to-all-start.4) | async-done | bytes 1048608 | tf_op jit(solution)/shard_map/all_to_all | solution.py:392
  146.2 2.1 constant_dynamic-slice_fusion.2
  148.3 4.4 %collective-permute-start.14 = (bf16[512,256]{1,0:T(8,128)(2,1)}, bf16[512,256]{1,0:T(8,128)(2,1)}, u32[]{:S(2)}, u32[]{:S(2)}) collective-permute-start(bf16[512,256]{1,0:T(8,128)(2,1)} %get-tuple-element.27), channel_id=1, source_target_pairs={{0,24},{8,16},{16,8},{24,0},{1,25},{9,17},{17,9},{25,1},{2,26},{10... | collective-permute-start | bytes 786440 | tf_op jit(solution)/shard_map/ppermute | solution.py:493
  152.7 31.7 %attend_backward.3 = bf16[2048,384]{1,0:T(8,128)(2,1)S(1)} custom-call(s32[16,10]{1,0:T(8,128)S(1)} %bitcast.25, s32[16]{0:T(128)S(1)} %bitcast.29, bf16[2048,384]{1,0:T(8,128)(2,1)} %bitcast.9.packed, bf16[2048,256]{1,0:T(8,128)(2,1)S(1)} %copy-done.10, bf16[2048,128]{1,0:T(8,128)(2,1)S(1)} %copy-done.15, f32[128,256]{1,0:T(8,128)S(1)} %get-tuple-element.21.stats), custom_call_target="tpu_custom_call" | custom-call | flops 53687091200 | bytes 3145728 | tf_op jit(solution)/shard_map/attend_backward/pallas_call | solution.py:303
  185.6 4.3 %all-to-all-start.3 = ((bf16[8,256,384]{2,1,0:T(8,128)(2,1)}), bf16[8,256,384]{2,1,0:T(8,128)(2,1)}, u32[]{:S(2)}, u32[]{:S(2)}) async-start(bf16[8,256,384]{2,1,0:T(8,128)(2,1)} %bitcast.18), calls=%async_computation.3 | async-start | bytes 3145728 | tf_op jit(solution)/shard_map/all_to_all | solution.py:392
  190.0 2.0 add_convert_fusion
  193.1 31.7 %attend_backward.2 = bf16[2048,384]{1,0:T(8,128)(2,1)S(1)} custom-call(s32[16,10]{1,0:T(8,128)S(1)} %bitcast.26, s32[16]{0:T(128)S(1)} %bitcast.30, bf16[2048,384]{1,0:T(8,128)(2,1)} %bitcast.5.packed, bf16[2048,256]{1,0:T(8,128)(2,1)S(1)} %copy-done.10, bf16[2048,128]{1,0:T(8,128)(2,1)S(1)} %copy-done.13, f32[128,256]{1,0:T(8,128)S(1)} %get-tuple-element.20.stats), custom_call_target="tpu_custom_call" | custom-call | flops 53687091200 | bytes 3145728 | tf_op jit(solution)/shard_map/attend_backward/pallas_call | solution.py:303
  226.0 25.0 %all_to_all.25.first = bf16[8,256,384]{2,1,0:T(8,128)(2,1)S(1)} all-to-all(bf16[8,256,384]{2,1,0:T(8,128)(2,1)} %bitcast.19), channel_id=1, replica_groups=mesh['fsdp'=4,'seq'=8] {'seq'}, dimensions={0} | all-to-all | bytes 3145728 | tf_op jit(solution)/shard_map/all_to_all | solution.py:392
  251.0 4.2 %unpack.1 = (bf16[256,2048]{1,0:T(8,128)(2,1)}, bf16[256,2048]{1,0:T(8,128)(2,1)}, bf16[256,2048]{1,0:T(8,128)(2,1)}) custom-call(bf16[8,256,384]{2,1,0:T(8,128)(2,1)S(1)} %all_to_all.25.first, bf16[8,256,384]{2,1,0:T(8,128)(2,1)} %all-to-all-done.3.second), custom_call_target="tpu_custom_call" | custom-call | tf_op jit(solution)/shard_map/unpack/pallas_call | solution.py:360
  256.8 3.6 %spread.1 = f32[512,2048]{1,0:T(8,128)} custom-call(bf16[8,512,256]{2,1,0:T(8,128)(2,1)S(1)} %bitcast.17), custom_call_target="tpu_custom_call" | custom-call | tf_op jit(solution)/shard_map/spread/pallas_call | solution.py:380
  (67 shorter events, 19.3 us)
Async XLA Ops:
  7.2 14.7 %copy-start = (bf16[512,2048]{1,0:T(8,128)(2,1)S(1)}, bf16[512,2048]{1,0:T(8,128)(2,1)}, u32[]{:S(2)}) copy-start(bf16[512,2048]{1,0:T(8,128)(2,1)} %param.11) | copy-start | bytes 6291460
  14.2 52.7 %all-to-all-start = ((bf16[8,256,384]{2,1,0:T(8,128)(2,1)}), bf16[8,256,384]{2,1,0:T(8,128)(2,1)}, u32[]{:S(2)}, u32[]{:S(2)}) async-start(bf16[8,256,384]{2,1,0:T(8,128)(2,1)} %copy-done.2), calls=%async_computation | async-start | bytes 3145728 | tf_op jit(solution)/shard_map/all_to_all | solution.py:392
  18.5 42.6 %collective-permute-start = (bf16[256,2048]{1,0:T(8,128)(2,1)}, bf16[256,2048]{1,0:T(8,128)(2,1)}, u32[]{:S(2)}, u32[]{:S(2)}) collective-permute-start(bf16[256,2048]{1,0:T(8,128)(2,1)} %bitcast.8.refs_1_), channel_id=1, source_target_pairs={{0,2},{1,3},{2,0},{3,1},{4,6},{5,7},{6,4},{7,5},{8,10},{9,11},{10,... | collective-permute-start | bytes 3145736 | tf_op jit(solution)/shard_map/ppermute | solution.py:411
  20.4 44.1 %collective-permute-start.1 = (bf16[256,2048]{1,0:T(8,128)(2,1)}, bf16[256,2048]{1,0:T(8,128)(2,1)}, u32[]{:S(2)}, u32[]{:S(2)}) collective-permute-start(bf16[256,2048]{1,0:T(8,128)(2,1)} %bitcast.8.refs_1_), channel_id=1, source_target_pairs={{0,4},{1,5},{2,6},{3,7},{4,0},{5,1},{6,2},{7,3},{8,12},{9,13},{10,... | collective-permute-start | bytes 3145736 | tf_op jit(solution)/shard_map/ppermute | solution.py:411
  23.0 65.3 %collective-permute-start.10 = (bf16[256,2048]{1,0:T(8,128)(2,1)}, bf16[256,2048]{1,0:T(8,128)(2,1)}, u32[]{:S(2)}, u32[]{:S(2)}) collective-permute-start(bf16[256,2048]{1,0:T(8,128)(2,1)} %constant_dynamic-slice_fusion.3.refs_11_), channel_id=1, source_target_pairs={{0,16},{1,17},{10,26},{11,27},{20,4},{21,5},{30,14},{31,15}} | collective-permute-start | bytes 3145736 | tf_op jit(solution)/shard_map/ppermute | solution.py:405
  24.7 63.9 %collective-permute-start.11 = (bf16[256,2048]{1,0:T(8,128)(2,1)}, bf16[256,2048]{1,0:T(8,128)(2,1)}, u32[]{:S(2)}, u32[]{:S(2)}) collective-permute-start(bf16[256,2048]{1,0:T(8,128)(2,1)} %constant_dynamic-slice_fusion.3.refs_11_), channel_id=1, source_target_pairs={{0,24},{1,25},{10,18},{11,19},{20,12},{21,13},{30,6},{31,7}} | collective-permute-start | bytes 3145736 | tf_op jit(solution)/shard_map/ppermute | solution.py:405
  26.0 62.8 %collective-permute-start.9 = (bf16[256,2048]{1,0:T(8,128)(2,1)}, bf16[256,2048]{1,0:T(8,128)(2,1)}, u32[]{:S(2)}, u32[]{:S(2)}) collective-permute-start(bf16[256,2048]{1,0:T(8,128)(2,1)} %constant_dynamic-slice_fusion.3.refs_11_), channel_id=1, source_target_pairs={{0,8},{1,9},{10,2},{11,3},{20,28},{21,29},{30,22},{31,23}} | collective-permute-start | bytes 3145736 | tf_op jit(solution)/shard_map/ppermute | solution.py:405
  63.0 26.1 %collective-permute-start.2 = (bf16[128,2048]{1,0:T(8,128)(2,1)}, bf16[128,2048]{1,0:T(8,128)(2,1)S(1)}, u32[]{:S(2)}, u32[]{:S(2)}) collective-permute-start(bf16[128,2048]{1,0:T(8,128)(2,1)} %slice.8), channel_id=1, source_target_pairs={{0,4},{1,5},{2,6},{3,7},{4,0},{5,1},{6,2},{7,3},{8,12},{9,13},{10,... | collective-permute-start | bytes 1572872 | tf_op jit(solution)/shard_map/ppermute | solution.py:411
  66.4 22.9 %collective-permute-start.3 = (bf16[128,2048]{1,0:T(8,128)(2,1)}, bf16[128,2048]{1,0:T(8,128)(2,1)S(1)}, u32[]{:S(2)}, u32[]{:S(2)}) collective-permute-start(bf16[128,2048]{1,0:T(8,128)(2,1)} %slice.9), channel_id=1, source_target_pairs={{0,2},{1,3},{2,0},{3,1},{4,6},{5,7},{6,4},{7,5},{8,10},{9,11},{10,... | collective-permute-start | bytes 1572872 | tf_op jit(solution)/shard_map/ppermute | solution.py:411
  66.9 29.8 %all-to-all-start.1 = ((bf16[8,256,384]{2,1,0:T(8,128)(2,1)}), bf16[8,256,384]{2,1,0:T(8,128)(2,1)}, u32[]{:S(2)}, u32[]{:S(2)}) async-start(bf16[8,256,384]{2,1,0:T(8,128)(2,1)} %get-tuple-element.17), calls=%async_computation.1 | async-start | bytes 3145728 | tf_op jit(solution)/shard_map/all_to_all | solution.py:392
  88.3 24.6 %collective-permute-start.4 = (bf16[256,2048]{1,0:T(8,128)(2,1)}, bf16[256,2048]{1,0:T(8,128)(2,1)}, u32[]{:S(2)}, u32[]{:S(2)}) collective-permute-start(bf16[256,2048]{1,0:T(8,128)(2,1)} %bitcast.8.refs_1_), channel_id=1, source_target_pairs={{0,1},{1,0},{2,3},{3,2},{4,5},{5,4},{6,7},{7,6},{8,9},{9,8},{10,11... | collective-permute-start | bytes 3145736 | tf_op jit(solution)/shard_map/ppermute | solution.py:411
  88.6 24.2 %collective-permute-start.5 = (bf16[256,2048]{1,0:T(8,128)(2,1)}, bf16[256,2048]{1,0:T(8,128)(2,1)}, u32[]{:S(2)}, u32[]{:S(2)}) collective-permute-start(bf16[256,2048]{1,0:T(8,128)(2,1)} %collective-permute-done.refs_2_), channel_id=1, source_target_pairs={{0,1},{1,0},{2,3},{3,2},{4,5},{5,4},{6,7},{7,6},{8,9},{9,8},{10,11... | collective-permute-start | bytes 3145736 | tf_op jit(solution)/shard_map/ppermute | solution.py:411
  88.8 24.1 %collective-permute-start.6 = (bf16[256,2048]{1,0:T(8,128)(2,1)}, bf16[256,2048]{1,0:T(8,128)(2,1)}, u32[]{:S(2)}, u32[]{:S(2)}) collective-permute-start(bf16[256,2048]{1,0:T(8,128)(2,1)} %collective-permute-done.1.refs_3_), channel_id=1, source_target_pairs={{0,1},{1,0},{2,3},{3,2},{4,5},{5,4},{6,7},{7,6},{8,9},{9,8},{10,11... | collective-permute-start | bytes 3145736 | tf_op jit(solution)/shard_map/ppermute | solution.py:411
  89.1 23.7 %collective-permute-start.7 = (bf16[128,2048]{1,0:T(8,128)(2,1)S(1)}, bf16[128,2048]{1,0:T(8,128)(2,1)}, u32[]{:S(2)}, u32[]{:S(2)}) collective-permute-start(bf16[128,2048]{1,0:T(8,128)(2,1)S(1)} %collective-permute-done.2.refs_4_), channel_id=1, source_target_pairs={{0,1},{1,0},{2,3},{3,2},{4,5},{5,4},{6,7},{7,6},{8,9},{9,8},{10,11... | collective-permute-start | bytes 1572872 | tf_op jit(solution)/shard_map/ppermute | solution.py:411
  89.3 23.5 %collective-permute-start.8 = (bf16[128,2048]{1,0:T(8,128)(2,1)S(1)}, bf16[128,2048]{1,0:T(8,128)(2,1)}, u32[]{:S(2)}, u32[]{:S(2)}) collective-permute-start(bf16[128,2048]{1,0:T(8,128)(2,1)S(1)} %collective-permute-done.3.refs_5_), channel_id=1, source_target_pairs={{0,1},{1,0},{2,3},{3,2},{4,5},{5,4},{6,7},{7,6},{8,9},{9,8},{10,11... | collective-permute-start | bytes 1572872 | tf_op jit(solution)/shard_map/ppermute | solution.py:411
  96.7 16.1 %copy-start.12 = (bf16[2048,128]{1,0:T(8,128)(2,1)S(1)}, bf16[2048,128]{1,0:T(8,128)(2,1)}, u32[]{:S(2)}) copy-start(bf16[2048,128]{1,0:T(8,128)(2,1)} %copy-done.11) | copy-start | bytes 1572868
  112.8 12.6 %copy-start.14 = (bf16[2048,128]{1,0:T(8,128)(2,1)}, bf16[2048,128]{1,0:T(8,128)(2,1)S(1)}, u32[]{:S(2)}) copy-start(bf16[2048,128]{1,0:T(8,128)(2,1)S(1)} %get-tuple-element.18.refs_16_.attn_out) | copy-start | bytes 1572868
  126.4 26.3 %copy-start.10 = (bf16[2048,256]{1,0:T(8,128)(2,1)S(1)}, bf16[2048,256]{1,0:T(8,128)(2,1)}, u32[]{:S(2)}) copy-start(bf16[2048,256]{1,0:T(8,128)(2,1)} %copy-done.9) | copy-start | bytes 3145732
  126.4 19.8 %all-to-all-start.4 = ((bf16[8,256,256]{2,1,0:T(8,128)(2,1)}), bf16[8,256,256]{2,1,0:T(8,128)(2,1)}, u32[]{:S(2)}, u32[]{:S(2)}) async-start(bf16[8,256,256]{2,1,0:T(8,128)(2,1)} %get-tuple-element.25), calls=%async_computation.4 | async-start | bytes 2097152 | tf_op jit(solution)/shard_map/all_to_all | solution.py:392
  148.3 41.7 %collective-permute-start.12 = (bf16[512,256]{1,0:T(8,128)(2,1)}, bf16[512,256]{1,0:T(8,128)(2,1)}, u32[]{:S(2)}, u32[]{:S(2)}) collective-permute-start(bf16[512,256]{1,0:T(8,128)(2,1)} %get-tuple-element.26), channel_id=1, source_target_pairs={{0,8},{8,0},{16,24},{24,16},{1,9},{9,1},{17,25},{25,17},{2,10},{10... | collective-permute-start | bytes 786440 | tf_op jit(solution)/shard_map/ppermute | solution.py:493
  148.3 41.7 %collective-permute-start.13 = (bf16[512,256]{1,0:T(8,128)(2,1)}, bf16[512,256]{1,0:T(8,128)(2,1)}, u32[]{:S(2)}, u32[]{:S(2)}) collective-permute-start(bf16[512,256]{1,0:T(8,128)(2,1)} %get-tuple-element.28), channel_id=1, source_target_pairs={{0,16},{8,24},{16,0},{24,8},{1,17},{9,25},{17,1},{25,9},{2,18},{10... | collective-permute-start | bytes 786440 | tf_op jit(solution)/shard_map/ppermute | solution.py:493
  148.3 41.7 %collective-permute-start.14 = (bf16[512,256]{1,0:T(8,128)(2,1)}, bf16[512,256]{1,0:T(8,128)(2,1)}, u32[]{:S(2)}, u32[]{:S(2)}) collective-permute-start(bf16[512,256]{1,0:T(8,128)(2,1)} %get-tuple-element.27), channel_id=1, source_target_pairs={{0,24},{8,16},{16,8},{24,0},{1,25},{9,17},{17,9},{25,1},{2,26},{10... | collective-permute-start | bytes 786440 | tf_op jit(solution)/shard_map/ppermute | solution.py:493
  185.6 40.4 %all-to-all-start.3 = ((bf16[8,256,384]{2,1,0:T(8,128)(2,1)}), bf16[8,256,384]{2,1,0:T(8,128)(2,1)}, u32[]{:S(2)}, u32[]{:S(2)}) async-start(bf16[8,256,384]{2,1,0:T(8,128)(2,1)} %bitcast.18), calls=%async_computation.3 | async-start | bytes 3145728 | tf_op jit(solution)/shard_map/all_to_all | solution.py:392
  189.9 65.3 %all-gather.3.cloned.1.call-start = ((), (), s32[]{:S(2)}) async-start(), calls=%async_computation.5 | async-start | bytes 2359296 | tf_op jit(solution)/shard_map/all_gather | solution.py:527
  (13 other events, 31.8 us)
Sparse Core Ops, SparseCore 0:
  192.6 33.8 all-gather.2

commit v3 on v0

--- a/solution.py
+++ b/solution.py
@@ -1,6 +1,11 @@
+import functools
+import math
+
 import jax
 import jax.numpy as jnp
 from jax import lax
+from jax.experimental import pallas as pl
+from jax.experimental.pallas import tpu as pltpu
 from jax.sharding import PartitionSpec as P
 
 HEADS = 32
@@ -118,7 +123,478 @@
     )
 
 
-def on_device(queries, keys, values, out_grad, out_weight, key_blocks, block_counts):
+PAIR = 2 * HD
+SCALE = HD ** (-0.5)
+BASE2 = SCALE * math.log2(math.e)
+
+
+def fold_rows(tile, combine):
+    return combine(tile.reshape(-1, 8, tile.shape[1]), axis=0)
+
+
+def block_rows(index, height=BLK):
+    return pl.ds(pl.multiple_of(index * height, height), height)
+
+
+def by_head(block):
+    first = lax.broadcasted_iota(jnp.int32, block.shape, 1) < HD
+    zero = jnp.zeros_like(block)
+    return jnp.concatenate([jnp.where(first, block, zero), jnp.where(first, zero, block)], axis=0)
+
+
+def by_head_t(block):
+    turned = block.T
+    first = lax.broadcasted_iota(jnp.int32, turned.shape, 0) < HD
+    zero = jnp.zeros_like(turned)
+    return jnp.concatenate([jnp.where(first, turned, zero), jnp.where(first, zero, turned)], axis=1)
+
+
+def own_parts(wide):
+    return jnp.concatenate([wide[:HD, :BLK], wide[HD:, BLK:]], axis=0)
+
+
+def columns(pair, part):
+    return pl.ds(PAIR * (3 * pair + part), PAIR)
+
+
+def dot(left, right):
+    return lax.dot_general(left, right, (((1,), (0,)), ((), ())), preferred_element_type=jnp.float32)
+
+
+def stack(source, places, right):
+    return dot(jnp.concatenate([source[at, :] for at in places], axis=0), right)
+
+
+def each_block(counts, begin, end, body):
+    @pl.loop(begin, end)
+    def _(index):
+        for slots in range(2, MAXK + 1):
+            @pl.when(counts[index] == slots)
+            def _():
+                body(index, slots)
+
+
+def forward_kernel(adjacency, counts, packed, first, second, stats, value_t, *, blocks):
+    outs = (first, second)
+
+    @pl.loop(0, blocks)
+    def _(index):
+        for pair in range(2):
+            value_t[pair, index] = packed[block_rows(index), columns(pair, 2)].T
+
+    def query_block(index, slots):
+        picked = [adjacency[index, slot] for slot in range(slots)]
+        places = [block_rows(block) for block in picked]
+        raws = [
+            stack(
+                packed.at[:, columns(pair, 1)],
+                places,
+                by_head_t(packed[block_rows(index), columns(pair, 0)]),
+            )
+            for pair in range(2)
+        ]
+        for pair, raw in enumerate(raws):
+            row_max = jnp.max(fold_rows(raw, jnp.max), axis=0, keepdims=True)
+            expo = jnp.exp2((raw - row_max) * BASE2)
+            row_sum = jnp.sum(fold_rows(expo, jnp.sum), axis=0, keepdims=True)
+            out_t = dot(
+                jnp.concatenate([value_t[pair, block] for block in picked], axis=1),
+                expo.astype(jnp.bfloat16),
+            )
+            outs[pair][block_rows(index), :] = own_parts(out_t / row_sum).T.astype(jnp.bfloat16)
+            stats[pair, block_rows(index, 8), :] = jnp.broadcast_to(
+                row_max * BASE2 + jnp.log2(row_sum), (8, 2 * BLK)
+            )
+
+    each_block(counts, 0, blocks, query_block)
+
+
+def backward_kernel(
+    adjacency, counts, packed, grad, attn_out, stats, *refs, blocks, begin, end
+):
+    query, key, value = (packed.at[:, pl.ds(PAIR * part, PAIR)] for part in range(3))
+    carried, rest = refs[: 3 if begin else 0], refs[3 if begin else 0 :]
+    outs, (key_t, key_sum, value_sum) = rest[:-3], rest[-3:]
+    query_g = outs[0]
+
+    @pl.loop(0, blocks)
+    def _(index):
+        key_t[index] = key[block_rows(index), :].T
+        if begin:
+            key_sum[block_rows(index), :] = carried[1][block_rows(index), :]
+            value_sum[block_rows(index), :] = carried[2][block_rows(index), :]
+        else:
+            key_sum[block_rows(index), :] = jnp.zeros((BLK, PAIR), jnp.float32)
+            value_sum[block_rows(index), :] = jnp.zeros((BLK, PAIR), jnp.float32)
+
+    def query_block(index, slots):
+        picked = [adjacency[index, slot] for slot in range(slots)]
+        query_rows = query[block_rows(index), :]
+        grad_rows = grad[block_rows(index), :]
+        queries, queries_t = by_head(query_rows), by_head_t(query_rows)
+        grads, grads_t = by_head(grad_rows), by_head_t(grad_rows)
+        stat = stats[0, pl.ds(pl.multiple_of(index * 8, 8), 1), :]
+        products = (
+            grad_rows.astype(jnp.float32) * attn_out[block_rows(index), :].astype(jnp.float32)
+        ).T
+        row_dot = jnp.concatenate(
+            [
+                jnp.sum(products[:HD], axis=0, keepdims=True),
+                jnp.sum(products[HD:], axis=0, keepdims=True),
+            ],
+            axis=1,
+        )
+        places = [block_rows(block) for block in picked]
+        prob = jnp.exp2(stack(key, places, queries_t) * BASE2 - stat)
+        term = (prob * (stack(value, places, grads_t) - row_dot)).astype(jnp.bfloat16)
+        key_terms = dot(term, queries)
+        value_terms = dot(prob.astype(jnp.bfloat16), grads)
+        for number, at in enumerate(places):
+            key_sum[at, :] += key_terms[BLK * number : BLK * (number + 1)]
+            value_sum[at, :] += value_terms[BLK * number : BLK * (number + 1)]
+        query_t = dot(jnp.concatenate([key_t[block] for block in picked], axis=1), term)
+        query_g[block_rows(index), :PAIR] = (own_parts(query_t).T * SCALE).astype(jnp.bfloat16)
+
+    each_block(counts, begin, end, query_block)
+    if end < blocks:
+        outs[1][...], outs[2][...] = key_sum[...], value_sum[...]
+    else:
+        if begin:
+            query_g[: BLK * begin, :PAIR] = carried[0][: BLK * begin, :]
+        query_g[:, PAIR : 2 * PAIR] = (key_sum[...] * SCALE).astype(jnp.bfloat16)
+        query_g[:, 2 * PAIR :] = value_sum[...].astype(jnp.bfloat16)
+
+
+VMEM = pl.BlockSpec(memory_space=pltpu.VMEM)
+SMEM = pl.BlockSpec(memory_space=pltpu.SMEM)
+PARAMS = pltpu.CompilerParams(vmem_limit_bytes=48 * 2**20)
+
+
+def cost(tokens, products):
+    tiles = tokens // BLK * MAXK * 2
+    return pl.CostEstimate(
+        flops=tiles * products * 2 * BLK * BLK * HD * 4,
+        bytes_accessed=12 * tokens * PAIR,
+        transcendentals=tiles * BLK * BLK,
+    )
+
+
+def forward(packed, adjacency, counts):
+    tokens = packed.shape[0]
+    blocks = tokens // BLK
+    return pl.pallas_call(
+        functools.partial(forward_kernel, blocks=blocks),
+        in_specs=[SMEM, SMEM, VMEM],
+        out_specs=[VMEM] * 3,
+        out_shape=[
+            jax.ShapeDtypeStruct((tokens, PAIR), jnp.bfloat16),
+            jax.ShapeDtypeStruct((tokens, PAIR), jnp.bfloat16),
+            jax.ShapeDtypeStruct((2, blocks * 8, 2 * BLK), jnp.float32),
+        ],
+        scratch_shapes=[pltpu.VMEM((2, blocks, PAIR, BLK), jnp.bfloat16)],
+        compiler_params=PARAMS,
+        cost_estimate=cost(tokens, 4),
+        name="attend_forward",
+    )(adjacency, counts, packed)
+
+
+def backward(packed, grad, pair, attn_out, stats, adjacency, counts, begin=0, end=None, carried=()):
+    tokens = packed.shape[0]
+    blocks = tokens // BLK
+    end = end or blocks
+    one = pl.BlockSpec((tokens, PAIR), lambda step: (0, 0))
+    three = pl.BlockSpec((tokens, 3 * PAIR), lambda step: (0, pair))
+    whole = pl.BlockSpec((tokens, 3 * PAIR), lambda step: (0, 0))
+    if end < blocks:
+        out_specs = [one] * 3
+        out_shape = [jax.ShapeDtypeStruct((tokens, PAIR), jnp.bfloat16)]
+        out_shape += [jax.ShapeDtypeStruct((tokens, PAIR), jnp.float32)] * 2
+    else:
+        out_specs = whole
+        out_shape = jax.ShapeDtypeStruct((tokens, 3 * PAIR), jnp.bfloat16)
+    return pl.pallas_call(
+        functools.partial(backward_kernel, blocks=blocks, begin=begin, end=end),
+        grid=(1,),
+        in_specs=[
+            SMEM, SMEM, three, pl.BlockSpec((tokens, PAIR), lambda step: (0, pair)), one,
+            pl.BlockSpec((1, blocks * 8, 2 * BLK), lambda step: (pair, 0, 0)),
+        ] + [one] * len(carried),
+        out_specs=out_specs,
+        out_shape=out_shape,
+        scratch_shapes=[
+            pltpu.VMEM((blocks, PAIR, BLK), jnp.bfloat16),
+            pltpu.VMEM((tokens, PAIR), jnp.float32),
+            pltpu.VMEM((tokens, PAIR), jnp.float32),
+        ],
+        compiler_params=PARAMS,
+        cost_estimate=cost(tokens * (end - begin) // blocks, 5),
+        name="attend_backward",
+    )(adjacency, counts, packed, grad, attn_out, stats, *carried)
+
+
+WIDE = pltpu.CompilerParams(vmem_limit_bytes=60 * 2**20)
+
+
+STEPS = 4
+
+
+def pack_kernel(queries, keys, values, weight, packed, own):
+    for group in range(packed.shape[0]):
+        for pair in range(2):
+            start = PAIR * (2 * group + pair)
+            for part, source in enumerate((queries, keys, values)):
+                packed[group, :, columns(pair, part)] = source[:, start : start + PAIR]
+    own[...] = weight[...]
+
+
+def pack(queries, keys, values, out_weight, groups):
+    tokens, width = queries.shape
+    height, share = tokens // STEPS, width // groups // STEPS
+
+    def weight_place(step):
+        skipped = lax.axis_index("seq") * (width // groups) % out_weight.shape[0]
+        return (skipped // share + step, 0)
+
+    taken = pl.BlockSpec((height, width), lambda step: (step, 0))
+    return pl.pallas_call(
+        pack_kernel,
+        grid=(STEPS,),
+        in_specs=[taken] * 3 + [pl.BlockSpec((share, width), weight_place)],
+        out_specs=[
+            pl.BlockSpec((groups, height, 6 * PAIR), lambda step: (0, step, 0)),
+            pl.BlockSpec((share, width), lambda step: (step, 0)),
+        ],
+        out_shape=[
+            jax.ShapeDtypeStruct((groups, tokens, 6 * PAIR), queries.dtype),
+            jax.ShapeDtypeStruct((width // groups, width), queries.dtype),
+        ],
+        compiler_params=WIDE,
+        name="pack",
+    )(queries, keys, values, out_weight)
+
+
+def unpack_kernel(first, second, query_g, key_g, value_g):
+    for group in range(first.shape[0]):
+        for pair, source in enumerate((first, second)):
+            start = PAIR * (2 * group + pair)
+            for part, out in enumerate((query_g, key_g, value_g)):
+                out[:, start : start + PAIR] = source[group, :, PAIR * part : PAIR * (part + 1)]
+
+
+def unpack(first, second):
+    groups, tokens, _ = first.shape
+    height = tokens // 4
+    taken = pl.BlockSpec((groups, height, 3 * PAIR), lambda step: (0, step, 0))
+    given = pl.BlockSpec((height, groups * 2 * PAIR), lambda step: (step, 0))
+    return pl.pallas_call(
+        unpack_kernel,
+        grid=(4,),
+        in_specs=[taken] * 2,
+        out_specs=[given] * 3,
+        out_shape=[jax.ShapeDtypeStruct((tokens, groups * 2 * PAIR), first.dtype)] * 3,
+        compiler_params=WIDE,
+        name="unpack",
+    )(first, second)
+
+
+def spread_kernel(*refs):
+    pieces, out = refs[:-1], refs[-1]
+    member = lax.axis_index("seq")
+    for mask, piece in enumerate(pieces):
+        width = piece.shape[1]
+        start = pl.multiple_of((member ^ mask) * width, width)
+        out[:, pl.ds(start, width)] = piece[...].astype(out.dtype)
+
+
+def spread(pieces):
+    rows, width = pieces[0].shape
+    height = rows // STEPS
+    return pl.pallas_call(
+        spread_kernel,
+        grid=(STEPS,),
+        in_specs=[pl.BlockSpec((height, width), lambda step: (step, 0))] * len(pieces),
+        out_specs=pl.BlockSpec((height, len(pieces) * width), lambda step: (step, 0)),
+        out_shape=jax.ShapeDtypeStruct((rows, len(pieces) * width), jnp.float32),
+        compiler_params=WIDE,
+        name="spread",
+    )(*pieces)
+
+
+def exchange(chunks):
+    return lax.all_to_all(chunks, "seq", split_axis=0, concat_axis=0, tiled=True)
+
+
+WEIGHT_ROUTES = (
+    ((0, 1), (1, 2), (2, 1), (3, 2)),
+    ((0, 2), (1, 3), (2, 0), (3, 1)),
+    ((2, 3), (1, 0), (2, 3), (1, 0)),
+)
+
+
+def send_weight(rows, step):
+    planes, members = lax.axis_size("fsdp"), lax.axis_size("seq")
+    routes = []
+    for member in range(members):
+        source, target = WEIGHT_ROUTES[step][member * planes // members]
+        routes.append((source * members + member, target * members + member))
+    return lax.ppermute(rows, ("fsdp", "seq"), routes)
+
+
+def swap(array, mask):
+    routes = [(s, s ^ mask) for s in range(lax.axis_size("seq"))]
+    return lax.ppermute(array, "seq", routes)
+
+
+def project_kernel(places, *refs):
+    pieces, rest = refs[: len(places)], refs[len(places) :]
+    weights, (first, second, attn_grad, terms) = rest[:4], rest[4:8]
+    whole, weight, landed, fetched = rest[8:]
+    plane, member = lax.axis_index("fsdp"), lax.axis_index("seq")
+    local = whole.shape[0] // terms.shape[0]
+    copies = []
+    for number, (mask, row) in enumerate(places):
+        start = pl.multiple_of((member ^ mask) * local + row, BLK)
+        target = whole.at[pl.ds(start, pieces[number].shape[0]), :]
+        copies.append(pltpu.make_async_copy(pieces[number], target, landed.at[number]))
+    for source, rows in enumerate(weights):
+        held = (plane == member // 2) if source == 0 else False
+        for home, (_, target) in enumerate(WEIGHT_ROUTES[source - 1] if source else ()):
+            held = held | ((member // 2 == home) & (plane == target))
+
+        @pl.when(held)
+        def _():
+            pltpu.make_async_copy(rows, weight, fetched).start()
+    for copy in copies:
+        copy.start()
+    pltpu.make_async_copy(weights[0], weight, fetched).wait()
+    for copy in copies:
+        copy.wait()
+    attn_t = jnp.concatenate([first[...].T, second[...].T], axis=0)
+    groups, _, width = terms.shape
+    for group in range(0, groups, 2):
+        wide = dot(attn_t, whole[:, width * group : width * (group + 2)]).astype(terms.dtype)
+        terms[group], terms[group + 1] = wide[:, :width], wide[:, width:]
+
+    @pl.loop(0, 4)
+    def _(part):
+        rows = block_rows(part, whole.shape[0] // 4)
+        attn_grad[rows, :] = lax.dot_general(
+            whole[rows, :], weight[...], (((1,), (1,)), ((), ())), preferred_element_type=jnp.float32
+        ).astype(attn_grad.dtype)
+
+
+def project(pieces, weights, first, second, groups):
+    places = [(mask, row) for mask, row, _ in pieces]
+    arrays = [piece for _, _, piece in pieces]
+    height, width = weights[0].shape
+    tokens = first.shape[0]
+    far = pl.BlockSpec(memory_space=pl.ANY)
+    return pl.pallas_call(
+        functools.partial(project_kernel, places),
+        in_specs=[far] * (len(arrays) + len(weights)) + [VMEM] * 2,
+        out_specs=[VMEM] * 2,
+        out_shape=[
+            jax.ShapeDtypeStruct((tokens, height), jnp.bfloat16),
+            jax.ShapeDtypeStruct((groups, height, width // groups), jnp.bfloat16),
+        ],
+        scratch_shapes=[
+            pltpu.VMEM((tokens, width), jnp.bfloat16),
+            pltpu.VMEM((height, width), jnp.bfloat16),
+            pltpu.SemaphoreType.DMA((len(arrays),)),
+            pltpu.SemaphoreType.DMA,
+        ],
+        compiler_params=PARAMS,
+        cost_estimate=pl.CostEstimate(
+            flops=4 * tokens * width * height,
+            bytes_accessed=2 * tokens * width + 8 * height * width,
+            transcendentals=0,
+        ),
+        name="project",
+    )(*arrays, *weights, first, second)
+
+
+def split_kernel(whole, *parts):
+    height = parts[0].shape[0]
+    for offset, part in enumerate(parts):
+        start = pl.multiple_of((lax.axis_index("fsdp") ^ offset) * height, height)
+        part[...] = whole[pl.ds(start, height), :]
+
+
+def split(whole, planes):
+    rows, width = whole.shape
+    return pl.pallas_call(
+        split_kernel,
+        in_specs=[VMEM],
+        out_specs=[VMEM] * planes,
+        out_shape=[jax.ShapeDtypeStruct((rows // planes, width), whole.dtype)] * planes,
+        compiler_params=PARAMS,
+        name="split",
+    )(whole)
+
+
+def fits_pairs(sizes):
+    planes, members = sizes["fsdp"], sizes["seq"]
+    return members == 8 and planes == 4 and members * 2 * PAIR == HEADS * HD
+
+
+def pair_device(queries, keys, values, out_grad, out_weight, key_blocks, block_counts):
+    planes, members = lax.axis_size("fsdp"), lax.axis_size("seq")
+    home = lax.axis_index("seq") // 2
+    local_tokens, model_width = queries.shape[1:]
+    tokens = local_tokens * members
+    adjacency, counts = key_blocks[0], block_counts[0]
+    shard = out_grad[0]
+
+    along, across = swap(shard, 2), swap(shard, 4)
+    chunks, own = pack(queries[0], keys[0], values[0], out_weight, members)
+    packed = exchange(chunks).reshape(tokens, 6 * PAIR)
+    near, far = send_weight(own, 0), send_weight(own, 1)
+    beside = swap(shard, 1)
+    packed, shard, near, far, along, across, beside = lax.optimization_barrier(
+        (packed, shard, near, far, along, across, beside)
+    )
+
+    last = send_weight(jnp.where((home == 1) | (home == 2), own, far), 2)
+    middle = local_tokens // 2
+    corner_top, corner_bottom = swap(along[:middle], 4), swap(across[middle:], 2)
+    beside = [beside, swap(along, 1), swap(across, 1)]
+    first, second, stats = forward(packed, adjacency, counts)
+    first, second, stats, corner_top, corner_bottom, *beside = lax.optimization_barrier(
+        (first, second, stats, corner_top, corner_bottom, *beside)
+    )
+    pieces = [(0, 0, shard), (2, 0, along), (4, 0, across)]
+    pieces += [(mask, 0, piece) for mask, piece in zip((1, 3, 5), beside)]
+    pieces += [(6, 0, corner_top), (6, middle, corner_bottom)]
+    pieces += [(7, 0, swap(corner_top, 1)), (7, middle, swap(corner_bottom, 1))]
+    attn_grad, by_columns = project(pieces, (own, near, far, last), first, second, members)
+
+    terms = exchange(by_columns).reshape(model_width, -1)
+    first_g = backward(packed, attn_grad, 0, first, stats, adjacency, counts)
+    first_g, terms = lax.optimization_barrier((first_g, terms))
+    parts = split(terms, planes)
+    received = [
+        lax.ppermute(parts[offset], "fsdp", [(z, z ^ offset) for z in range(planes)])
+        for offset in range(1, planes)
+    ]
+    first_r = exchange(first_g.reshape(members, local_tokens, 3 * PAIR))
+    split_at = tokens // BLK // 2
+    started = backward(
+        packed, attn_grad, 1, second, stats, adjacency, counts, end=split_at
+    )
+    *started, received = lax.optimization_barrier((*started, received))
+    summed = sum(part.astype(jnp.float32) for part in [parts[0], *received]).astype(terms.dtype)
+    sides = [summed, swap(summed, 2), swap(summed, 4), swap(summed, 6)]
+    second_g = backward(
+        packed, attn_grad, 1, second, stats, adjacency, counts, begin=split_at, carried=started
+    )
+    second_g, *sides = lax.optimization_barrier((second_g, *sides))
+    wo_grad = spread([part for one in sides for part in (one, swap(one, 1))])
+    second_r = exchange(second_g.reshape(members, local_tokens, 3 * PAIR))
+    query_g, key_g, value_g = unpack(first_r, second_r)
+    return (query_g[None], key_g[None], value_g[None], wo_grad)
+
+
+def general_device(queries, keys, values, out_grad, out_weight, key_blocks, block_counts):
     local_tokens = queries.shape[1]
     model_width = queries.shape[2]
     seq_devices = lax.axis_size("seq")
@@ -179,9 +655,13 @@
     return (to_tokens(query_t), to_tokens(key_t), to_tokens(value_t), wo_grad)
 
 
+def on_device(mesh):
+    return pair_device if fits_pairs(mesh.shape) else general_device
+
+
 def solution(mesh):
     return jax.shard_map(
-        on_device,
+        on_device(mesh),
         mesh=mesh,
         in_specs=(
             P("fsdp", "seq", None),

time: 1140 us -> 213 us (0.19); the launches traced: 1130 us -> 212 us
  local copies, waits for them, and re-layouts: 349 us -> 7.76 us
  matrix products: 258 us -> 0 us
  waiting for transfers between devices: 262 us -> 84.5 us
  other arithmetic: 133 us -> 1.54 us
  Pallas kernels: 0 us -> 77.7 us
  loops' own time: 59.5 us -> 0 us
  blocking collectives: 19.6 us -> 0 us
  between operations: 14.5 us -> 0.94 us
    dot_general x72 -> x0, matrix products: 258 us -> none  [the longest x10 59.6 us: output_step(): jnp.einsum('ihqk,ikhd->iqhd', prob_half, value_heads[picked], preferred_e...]
    gather x60 -> x0, local copies, waits for them, and re-layouts: 250 us -> none  [the longest x20 75.4 us: grad_step(): chosen_keys = key_heads[picked]]
    reduce_scatter x1 -> x0, waiting for transfers between devices: 178 us -> none  [on_device(): lax.psum_scatter(lax.dot_general(attn_out, loss_grad, (((0,), (0,)), ((),...]
    scatter-add x20 -> x0, other arithmetic: 104 us -> none  [the longest x10 52 us: grad_step(): value_accum = value_accum.at[picked].add(value_terms)]
    pallas_call x0 -> x9, Pallas kernels: none -> 77.7 us  [the longest x3 37.2 us: backward(): pl.pallas_call(functools.partial(backward_kernel, blocks=blocks, begin=be...]
    ppermute x0 -> x22, waiting for transfers between devices: none -> 71.9 us  [the longest x16 55 us: swap(): return lax.ppermute(array, 'seq', routes)]
    another operation x3 -> x0, loops' own time: 59.5 us -> none  [the longest x1 20 us: head_forward(): lax.scan(stat_step, (start_max, start_sum), jnp.arange(MAXK))]
    unnamed x36 -> x41, local copies, waits for them, and re-layouts: 49.5 us -> 5.13 us
  transfers between devices with their start and end apart: 10 -> 26, of which waited for: 8 -> 9; matrix products, arithmetic and copies ran while one was open for 61% -> 1% of each run, Pallas kernels for 0% -> 28%
where the time goes in v3:
time: 213 us; the launch traced here: 212 us
  waiting for transfers between devices  84.5 us (40%)
  Pallas kernels  77.7 us (36%)
  starting transfers between devices  39.8 us (19%)
  local copies, waits for them, and re-layouts  7.76 us (4%)
    ppermute x16, waiting for transfers between devices, swap(): return lax.ppermute(array, 'seq', routes)  55 us
    pallas_call x3, Pallas kernels, backward(): pl.pallas_call(functools.partial(backward_kernel, blocks=blocks, begin=be...  37.2 us
    pallas_call x1, Pallas kernels, forward(): pl.pallas_call(functools.partial(forward_kernel, blocks=blocks), in_specs...  18.2 us
    all_to_all x4, starting transfers between devices, exchange(): lax.all_to_all(chunks, 'seq', split_axis=0, concat_axis=0, tiled=True)  16.3 us
    ppermute x3, waiting for transfers between devices, pair_device(): lax.ppermute(parts[offset], 'fsdp', [(z, z ^ offset) for z in range(plane...  13.8 us
    all_to_all x4, waiting for transfers between devices, exchange(): lax.all_to_all(chunks, 'seq', split_axis=0, concat_axis=0, tiled=True)  12.6 us
    ppermute x16, starting transfers between devices, swap(): return lax.ppermute(array, 'seq', routes)  11.5 us
    pallas_call x1, Pallas kernels, project(): pl.pallas_call(functools.partial(project_kernel, places), in_specs=[far]...  8.83 us
  transfers between devices with their start and end apart: 26, of which 9 were waited for; matrix products, arithmetic and copies ran while one was open for 1% of the time, Pallas kernels for 28%

profile of v3, /device:TPU:16, one launch (start us, length us, event | category | flops | bytes accessed | tf_op | source)
XLA Modules:
  0.0 212.2 jit_solution(902102622126327845)
XLA Ops:
  0.6 4.8 %pack.1 = (bf16[8,256,768]{2,1,0:T(8,128)(2,1)}, bf16[256,2048]{1,0:T(8,128)(2,1)}) custom-call(bf16[256,2048]{1,0:T(8,128)(2,1)} %bitcast.26, bf16[256,2048]{1,0:T(8,128)(2,1)} %bitcast.27, bf16[256,2048]{1,0:T(8,128)(2,1)} %bitcast.28, bf16[512,2048]{1,0:T(8,128)(2,1)} %weight.1), custom_call_target="tpu_custom_call" | custom-call | tf_op jit(solution)/shard_map/pack/pallas_call | solution.py:359
  5.4 3.9 %all-to-all-start = ((bf16[8,256,768]{2,1,0:T(8,128)(2,1)}), bf16[8,256,768]{2,1,0:T(8,128)(2,1)S(1)}, u32[]{:S(2)}, u32[]{:S(2)}) async-start(bf16[8,256,768]{2,1,0:T(8,128)(2,1)} %get-tuple-element.49), calls=%async_computation | async-start | bytes 6291456 | tf_op jit(solution)/shard_map/all_to_all | solution.py:424
  9.8 1.7 collective-permute-start.3
  14.2 1.7 collective-permute-start
  16.0 52.8 %collective-permute-done.3.refs_2_ = bf16[256,2048]{1,0:T(8,128)(2,1)} collective-permute-done((bf16[256,2048]{1,0:T(8,128)(2,1)}, bf16[256,2048]{1,0:T(8,128)(2,1)}, u32[]{:S(2)}, u32[]{:S(2)}) %collective-permute-start.3) | collective-permute-done | bytes 1048608 | tf_op jit(solution)/shard_map/ppermute | solution.py:445
  68.9 1.5 slice.6
  75.7 3.5 %collective-permute-start.11 = (bf16[256,2048]{1,0:T(8,128)(2,1)S(1)}, bf16[256,2048]{1,0:T(8,128)(2,1)S(1)}, u32[]{:S(2)}, u32[]{:S(2)}) collective-permute-start(bf16[256,2048]{1,0:T(8,128)(2,1)S(1)} %broadcast_select_fusion), channel_id=1, source_target_pairs={{16,24},{17,25},{10,2},{11,3},{20,28},{21,29},{14,6},{15,7}} | collective-permute-start | bytes 3145736 | tf_op jit(solution)/shard_map/ppermute | solution.py:440
  79.2 18.2 %attend_forward.1 = (bf16[2048,128]{1,0:T(8,128)(2,1)S(1)}, bf16[2048,128]{1,0:T(8,128)(2,1)S(1)}, f32[2,128,256]{2,1,0:T(8,128)S(1)}) custom-call(s32[16,10]{1,0:T(8,128)S(1)} %bitcast.18, s32[16]{0:T(128)S(1)} %bitcast.22, bf16[2048,768]{1,0:T(8,128)(2,1)S(1)} %bitcast.14), custom_call_target="tpu_custom_call" | custom-call | flops 10737418240 | bytes 3145728 | tf_op jit(solution)/shard_map/attend_forward/pallas_call | solution.py:285
  98.1 3.2 %collective-permute-done.11.refs_13_ = bf16[256,2048]{1,0:T(8,128)(2,1)S(1)} collective-permute-done((bf16[256,2048]{1,0:T(8,128)(2,1)S(1)}, bf16[256,2048]{1,0:T(8,128)(2,1)S(1)}, u32[]{:S(2)}, u32[]{:S(2)}) %collective-permute-start.11) | collective-permute-done | bytes 1048608 | tf_op jit(solution)/shard_map/ppermute | solution.py:440
  102.2 8.8 %project.1 = (bf16[2048,256]{1,0:T(8,128)(2,1)S(1)}, bf16[8,256,256]{2,1,0:T(8,128)(2,1)}) custom-call(bf16[256,2048]{1,0:T(8,128)(2,1)} %bitcast.32, bf16[256,2048]{1,0:T(8,128)(2,1)} %collective-permute-done.2.refs_1_, bf16[256,2048]{1,0:T(8,128)(2,1)} %collective-permute-done.3.refs_2_, bf16[256,2048]{1,0:T(8,128)(2,1)} %collective-permute-done.4.refs_3_, ...), custom_call_target="tpu_custom_call" | custom-call | flops 4294967296 | bytes 12582912 | tf_op jit(solution)/shard_map/project/pallas_call | solution.py:492
  111.1 3.9 %all-to-all-start.1 = ((bf16[8,256,256]{2,1,0:T(8,128)(2,1)}), bf16[8,256,256]{2,1,0:T(8,128)(2,1)S(1)}, u32[]{:S(2)}, u32[]{:S(2)}) async-start(bf16[8,256,256]{2,1,0:T(8,128)(2,1)} %get-tuple-element.70), calls=%async_computation.1 | async-start | bytes 2097152 | tf_op jit(solution)/shard_map/all_to_all | solution.py:424
  115.0 17.1 %attend_backward.3 = bf16[2048,384]{1,0:T(8,128)(2,1)} custom-call(s32[16,10]{1,0:T(8,128)S(1)} %bitcast.19, s32[16]{0:T(128)S(1)} %bitcast.23, bf16[2048,768]{1,0:T(8,128)(2,1)} %bitcast.15, bf16[2048,256]{1,0:T(8,128)(2,1)S(1)} %get-tuple-element.68.grad, bf16[2048,128]{1,0:T(8,128)(2,1)S(1)} %copy-done.5, f32[2,128,256]{2,1,0:T(8,128)S(1)} %get-tuple-element.69.stats), custom_call_target="tpu_custom_call" | custom-call | flops 13421772800 | bytes 3145728 | tf_op jit(solution)/shard_map/attend_backward/pallas_call | solution.py:315
  132.0 4.5 %all-to-all-start.2 = ((bf16[8,256,384]{2,1,0:T(8,128)(2,1)}), bf16[8,256,384]{2,1,0:T(8,128)(2,1)}, u32[]{:S(2)}, u32[]{:S(2)}) async-start(bf16[8,256,384]{2,1,0:T(8,128)(2,1)} %bitcast.8), calls=%async_computation.2 | async-start | bytes 3145728 | tf_op jit(solution)/shard_map/all_to_all | solution.py:424
  136.6 4.0 %collective-permute-start.12 = (bf16[512,256]{1,0:T(8,128)(2,1)S(1)}, bf16[512,256]{1,0:T(8,128)(2,1)S(1)}, u32[]{:S(2)}, u32[]{:S(2)}) collective-permute-start(bf16[512,256]{1,0:T(8,128)(2,1)S(1)} %get-tuple-element.76), channel_id=1, source_target_pairs={{0,8},{8,0},{16,24},{24,16},{1,9},{9,1},{17,25},{25,17},{2,10},{10... | collective-permute-start | bytes 786440 | tf_op jit(solution)/shard_map/ppermute | solution.py:576
  140.6 1.5 collective-permute-start.14
  143.2 8.4 %attend_backward.4 = (bf16[2048,128]{1,0:T(8,128)(2,1)S(1)}, f32[2048,128]{1,0:T(8,128)S(1)}, f32[2048,128]{1,0:T(8,128)S(1)}) custom-call(s32[16,10]{1,0:T(8,128)S(1)} %bitcast.20, s32[16]{0:T(128)S(1)} %bitcast.24, bf16[2048,768]{1,0:T(8,128)(2,1)} %bitcast.16, bf16[2048,256]{1,0:T(8,128)(2,1)S(1)} %get-tuple-element.68.grad, ...), custom_call_target="tpu_custom_call" | custom-call | flops 6710886400 | bytes 1572864 | tf_op jit(solution)/shard_map/attend_backward/pallas_call | solution.py:315
  151.7 6.9 %collective-permute-done.13 = bf16[512,256]{1,0:T(8,128)(2,1)S(1)} collective-permute-done((bf16[512,256]{1,0:T(8,128)(2,1)S(1)}, bf16[512,256]{1,0:T(8,128)(2,1)S(1)}, u32[]{:S(2)}, u32[]{:S(2)}) %collective-permute-start.13) | collective-permute-done | bytes 262176 | tf_op jit(solution)/shard_map/ppermute | solution.py:576
  158.6 6.9 %collective-permute-done.14 = bf16[512,256]{1,0:T(8,128)(2,1)S(1)} collective-permute-done((bf16[512,256]{1,0:T(8,128)(2,1)S(1)}, bf16[512,256]{1,0:T(8,128)(2,1)S(1)}, u32[]{:S(2)}, u32[]{:S(2)}) %collective-permute-start.14) | collective-permute-done | bytes 262176 | tf_op jit(solution)/shard_map/ppermute | solution.py:576
  165.6 2.7 %collective-permute-start.17 = (bf16[512,256]{1,0:T(8,128)(2,1)S(1)}, bf16[512,256]{1,0:T(8,128)(2,1)S(1)}, u32[]{:S(2)}, u32[]{:S(2)}) collective-permute-start(bf16[512,256]{1,0:T(8,128)(2,1)S(1)} %add_convert_fusion.refs_0_), channel_id=1, source_target_pairs={{0,6},{1,7},{2,4},{3,5},{4,2},{5,3},{6,0},{7,1},{8,14},{9,15},{10,... | collective-permute-start | bytes 786440 | tf_op jit(solution)/shard_map/ppermute | solution.py:445
  169.1 11.7 %attend_backward.5 = bf16[2048,384]{1,0:T(8,128)(2,1)} custom-call(s32[16,10]{1,0:T(8,128)S(1)} %bitcast.21, s32[16]{0:T(128)S(1)} %bitcast.25, bf16[2048,768]{1,0:T(8,128)(2,1)} %bitcast.17, bf16[2048,256]{1,0:T(8,128)(2,1)S(1)} %get-tuple-element.68.grad, bf16[2048,128]{1,0:T(8,128)(2,1)S(1)} %copy-done.3, f32[2,128,256]{2,1,0:T(8,128)S(1)} %get-tuple-element.69.stats, ...), custom_call_target="tpu_custom_call" | custom-call | flops 6710886400 | bytes 1572864 | tf_op jit(solution)/shard_map/attend_backward/pallas_call | solution.py:315
  181.7 4.0 %all-to-all-start.3 = ((bf16[8,256,384]{2,1,0:T(8,128)(2,1)}), bf16[8,256,384]{2,1,0:T(8,128)(2,1)S(1)}, u32[]{:S(2)}, u32[]{:S(2)}) async-start(bf16[8,256,384]{2,1,0:T(8,128)(2,1)} %bitcast.9), calls=%async_computation.3 | async-start | bytes 3145728 | tf_op jit(solution)/shard_map/all_to_all | solution.py:424
  189.9 4.2 %spread.1 = f32[512,2048]{1,0:T(8,128)} custom-call(bf16[512,256]{1,0:T(8,128)(2,1)} %copy-done.7, bf16[512,256]{1,0:T(8,128)(2,1)} %copy-done.12, bf16[512,256]{1,0:T(8,128)(2,1)} %collective-permute-done.15.refs_2_, bf16[512,256]{1,0:T(8,128)(2,1)} %copy-done.13, bf16[512,256]{1,0:T(8,128)(2,1)} %copy-done.10, bf16[512,256]{1,0:T(8,128)(2,1)} %copy-done.14, ...), custom_call_target="tpu_custom_call" | custom-call | tf_op jit(solution)/shard_map/spread/pallas_call | solution.py:412
  194.1 12.6 %all-to-all-done.3.second = bf16[8,256,384]{2,1,0:T(8,128)(2,1)S(1)} async-done(((bf16[8,256,384]{2,1,0:T(8,128)(2,1)}), bf16[8,256,384]{2,1,0:T(8,128)(2,1)S(1)}, u32[]{:S(2)}, u32[]{:S(2)}) %all-to-all-start.3) | async-done | bytes 1572896 | tf_op jit(solution)/shard_map/all_to_all | solution.py:424
  207.8 4.4 %unpack.1 = (bf16[256,2048]{1,0:T(8,128)(2,1)}, bf16[256,2048]{1,0:T(8,128)(2,1)}, bf16[256,2048]{1,0:T(8,128)(2,1)}) custom-call(bf16[8,256,384]{2,1,0:T(8,128)(2,1)} %all-to-all-done.2.first, bf16[8,256,384]{2,1,0:T(8,128)(2,1)} %copy-done.6), custom_call_target="tpu_custom_call" | custom-call | tf_op jit(solution)/shard_map/unpack/pallas_call | solution.py:389
  (82 shorter events, 18.5 us)
Async XLA Ops:
  5.4 63.5 %all-to-all-start = ((bf16[8,256,768]{2,1,0:T(8,128)(2,1)}), bf16[8,256,768]{2,1,0:T(8,128)(2,1)S(1)}, u32[]{:S(2)}, u32[]{:S(2)}) async-start(bf16[8,256,768]{2,1,0:T(8,128)(2,1)} %get-tuple-element.49), calls=%async_computation | async-start | bytes 6291456 | tf_op jit(solution)/shard_map/all_to_all | solution.py:424
  9.3 6.7 %collective-permute-start.4 = (bf16[256,2048]{1,0:T(8,128)(2,1)}, bf16[256,2048]{1,0:T(8,128)(2,1)}, u32[]{:S(2)}, u32[]{:S(2)}) collective-permute-start(bf16[256,2048]{1,0:T(8,128)(2,1)} %bitcast.29), channel_id=1, source_target_pairs={{0,1},{1,0},{2,3},{3,2},{4,5},{5,4},{6,7},{7,6},{8,9},{9,8},{10,11... | collective-permute-start | bytes 3145736 | tf_op jit(solution)/shard_map/ppermute | solution.py:445
  9.8 59.0 %collective-permute-start.3 = (bf16[256,2048]{1,0:T(8,128)(2,1)}, bf16[256,2048]{1,0:T(8,128)(2,1)}, u32[]{:S(2)}, u32[]{:S(2)}) collective-permute-start(bf16[256,2048]{1,0:T(8,128)(2,1)} %bitcast.30), channel_id=1, source_target_pairs={{0,4},{1,5},{2,6},{3,7},{4,0},{5,1},{6,2},{7,3},{8,12},{9,13},{10,... | collective-permute-start | bytes 3145736 | tf_op jit(solution)/shard_map/ppermute | solution.py:445
  11.5 57.4 %collective-permute-start.2 = (bf16[256,2048]{1,0:T(8,128)(2,1)}, bf16[256,2048]{1,0:T(8,128)(2,1)}, u32[]{:S(2)}, u32[]{:S(2)}) collective-permute-start(bf16[256,2048]{1,0:T(8,128)(2,1)} %bitcast.31), channel_id=1, source_target_pairs={{0,2},{1,3},{2,0},{3,1},{4,6},{5,7},{6,4},{7,5},{8,10},{9,11},{10,... | collective-permute-start | bytes 3145736 | tf_op jit(solution)/shard_map/ppermute | solution.py:445
  13.0 55.9 %collective-permute-start.1 = (bf16[256,2048]{1,0:T(8,128)(2,1)}, bf16[256,2048]{1,0:T(8,128)(2,1)}, u32[]{:S(2)}, u32[]{:S(2)}) collective-permute-start(bf16[256,2048]{1,0:T(8,128)(2,1)} %get-tuple-element.50.refs_10_), channel_id=1, source_target_pairs={{0,16},{1,17},{10,26},{11,27},{20,4},{21,5},{30,14},{31,15}} | collective-permute-start | bytes 3145736 | tf_op jit(solution)/shard_map/ppermute | solution.py:440
  14.2 54.7 %collective-permute-start = (bf16[256,2048]{1,0:T(8,128)(2,1)}, bf16[256,2048]{1,0:T(8,128)(2,1)}, u32[]{:S(2)}, u32[]{:S(2)}) collective-permute-start(bf16[256,2048]{1,0:T(8,128)(2,1)} %get-tuple-element.50.refs_10_), channel_id=1, source_target_pairs={{0,8},{1,9},{10,18},{11,19},{20,12},{21,13},{30,22},{31,23}} | collective-permute-start | bytes 3145736 | tf_op jit(solution)/shard_map/ppermute | solution.py:440
  70.5 26.9 %collective-permute-start.7 = (bf16[256,2048]{1,0:T(8,128)(2,1)}, bf16[256,2048]{1,0:T(8,128)(2,1)S(1)}, u32[]{:S(2)}, u32[]{:S(2)}) collective-permute-start(bf16[256,2048]{1,0:T(8,128)(2,1)} %collective-permute-done.2.refs_1_), channel_id=1, source_target_pairs={{0,1},{1,0},{2,3},{3,2},{4,5},{5,4},{6,7},{7,6},{8,9},{9,8},{10,11... | collective-permute-start | bytes 3145736 | tf_op jit(solution)/shard_map/ppermute | solution.py:445
  71.7 25.8 %collective-permute-start.8 = (bf16[256,2048]{1,0:T(8,128)(2,1)}, bf16[256,2048]{1,0:T(8,128)(2,1)S(1)}, u32[]{:S(2)}, u32[]{:S(2)}) collective-permute-start(bf16[256,2048]{1,0:T(8,128)(2,1)} %collective-permute-done.3.refs_2_), channel_id=1, source_target_pairs={{0,1},{1,0},{2,3},{3,2},{4,5},{5,4},{6,7},{7,6},{8,9},{9,8},{10,11... | collective-permute-start | bytes 3145736 | tf_op jit(solution)/shard_map/ppermute | solution.py:445
  72.2 25.2 %collective-permute-start.6 = (bf16[128,2048]{1,0:T(8,128)(2,1)S(1)}, bf16[128,2048]{1,0:T(8,128)(2,1)S(1)}, u32[]{:S(2)}, u32[]{:S(2)}) collective-permute-start(bf16[128,2048]{1,0:T(8,128)(2,1)S(1)} %slice.7), channel_id=1, source_target_pairs={{0,2},{1,3},{2,0},{3,1},{4,6},{5,7},{6,4},{7,5},{8,10},{9,11},{10,... | collective-permute-start | bytes 1572872 | tf_op jit(solution)/shard_map/ppermute | solution.py:445
  73.6 23.8 %collective-permute-start.5 = (bf16[128,2048]{1,0:T(8,128)(2,1)S(1)}, bf16[128,2048]{1,0:T(8,128)(2,1)S(1)}, u32[]{:S(2)}, u32[]{:S(2)}) collective-permute-start(bf16[128,2048]{1,0:T(8,128)(2,1)S(1)} %slice.6), channel_id=1, source_target_pairs={{0,4},{1,5},{2,6},{3,7},{4,0},{5,1},{6,2},{7,3},{8,12},{9,13},{10,... | collective-permute-start | bytes 1572872 | tf_op jit(solution)/shard_map/ppermute | solution.py:445
  75.7 25.6 %collective-permute-start.11 = (bf16[256,2048]{1,0:T(8,128)(2,1)S(1)}, bf16[256,2048]{1,0:T(8,128)(2,1)S(1)}, u32[]{:S(2)}, u32[]{:S(2)}) collective-permute-start(bf16[256,2048]{1,0:T(8,128)(2,1)S(1)} %broadcast_select_fusion), channel_id=1, source_target_pairs={{16,24},{17,25},{10,2},{11,3},{20,28},{21,29},{14,6},{15,7}} | collective-permute-start | bytes 3145736 | tf_op jit(solution)/shard_map/ppermute | solution.py:440
  97.5 3.7 %collective-permute-start.9 = (bf16[128,2048]{1,0:T(8,128)(2,1)S(1)}, bf16[128,2048]{1,0:T(8,128)(2,1)S(1)}, u32[]{:S(2)}, u32[]{:S(2)}) collective-permute-start(bf16[128,2048]{1,0:T(8,128)(2,1)S(1)} %collective-permute-done.5.refs_6_), channel_id=1, source_target_pairs={{0,1},{1,0},{2,3},{3,2},{4,5},{5,4},{6,7},{7,6},{8,9},{9,8},{10,11... | collective-permute-start | bytes 1572872 | tf_op jit(solution)/shard_map/ppermute | solution.py:445
  97.6 3.7 %collective-permute-start.10 = (bf16[128,2048]{1,0:T(8,128)(2,1)S(1)}, bf16[128,2048]{1,0:T(8,128)(2,1)S(1)}, u32[]{:S(2)}, u32[]{:S(2)}) collective-permute-start(bf16[128,2048]{1,0:T(8,128)(2,1)S(1)} %collective-permute-done.6.refs_7_), channel_id=1, source_target_pairs={{0,1},{1,0},{2,3},{3,2},{4,5},{5,4},{6,7},{7,6},{8,9},{9,8},{10,11... | collective-permute-start | bytes 1572872 | tf_op jit(solution)/shard_map/ppermute | solution.py:445
  111.1 21.0 %all-to-all-start.1 = ((bf16[8,256,256]{2,1,0:T(8,128)(2,1)}), bf16[8,256,256]{2,1,0:T(8,128)(2,1)S(1)}, u32[]{:S(2)}, u32[]{:S(2)}) async-start(bf16[8,256,256]{2,1,0:T(8,128)(2,1)} %get-tuple-element.70), calls=%async_computation.1 | async-start | bytes 2097152 | tf_op jit(solution)/shard_map/all_to_all | solution.py:424
  132.0 49.6 %all-to-all-start.2 = ((bf16[8,256,384]{2,1,0:T(8,128)(2,1)}), bf16[8,256,384]{2,1,0:T(8,128)(2,1)}, u32[]{:S(2)}, u32[]{:S(2)}) async-start(bf16[8,256,384]{2,1,0:T(8,128)(2,1)} %bitcast.8), calls=%async_computation.2 | async-start | bytes 3145728 | tf_op jit(solution)/shard_map/all_to_all | solution.py:424
  136.6 15.1 %collective-permute-start.12 = (bf16[512,256]{1,0:T(8,128)(2,1)S(1)}, bf16[512,256]{1,0:T(8,128)(2,1)S(1)}, u32[]{:S(2)}, u32[]{:S(2)}) collective-permute-start(bf16[512,256]{1,0:T(8,128)(2,1)S(1)} %get-tuple-element.76), channel_id=1, source_target_pairs={{0,8},{8,0},{16,24},{24,16},{1,9},{9,1},{17,25},{25,17},{2,10},{10... | collective-permute-start | bytes 786440 | tf_op jit(solution)/shard_map/ppermute | solution.py:576
  140.6 17.9 %collective-permute-start.13 = (bf16[512,256]{1,0:T(8,128)(2,1)S(1)}, bf16[512,256]{1,0:T(8,128)(2,1)S(1)}, u32[]{:S(2)}, u32[]{:S(2)}) collective-permute-start(bf16[512,256]{1,0:T(8,128)(2,1)S(1)} %get-tuple-element.77), channel_id=1, source_target_pairs={{0,16},{8,24},{16,0},{24,8},{1,17},{9,25},{17,1},{25,9},{2,18},{10... | collective-permute-start | bytes 786440 | tf_op jit(solution)/shard_map/ppermute | solution.py:576
  140.6 24.8 %collective-permute-start.14 = (bf16[512,256]{1,0:T(8,128)(2,1)S(1)}, bf16[512,256]{1,0:T(8,128)(2,1)S(1)}, u32[]{:S(2)}, u32[]{:S(2)}) collective-permute-start(bf16[512,256]{1,0:T(8,128)(2,1)S(1)} %get-tuple-element.78), channel_id=1, source_target_pairs={{0,24},{8,16},{16,8},{24,0},{1,25},{9,17},{17,9},{25,1},{2,26},{10... | collective-permute-start | bytes 786440 | tf_op jit(solution)/shard_map/ppermute | solution.py:576
  165.6 15.3 %collective-permute-start.17 = (bf16[512,256]{1,0:T(8,128)(2,1)S(1)}, bf16[512,256]{1,0:T(8,128)(2,1)S(1)}, u32[]{:S(2)}, u32[]{:S(2)}) collective-permute-start(bf16[512,256]{1,0:T(8,128)(2,1)S(1)} %add_convert_fusion.refs_0_), channel_id=1, source_target_pairs={{0,6},{1,7},{2,4},{3,5},{4,2},{5,3},{6,0},{7,1},{8,14},{9,15},{10,... | collective-permute-start | bytes 786440 | tf_op jit(solution)/shard_map/ppermute | solution.py:445
  168.2 12.6 %collective-permute-start.16 = (bf16[512,256]{1,0:T(8,128)(2,1)S(1)}, bf16[512,256]{1,0:T(8,128)(2,1)S(1)}, u32[]{:S(2)}, u32[]{:S(2)}) collective-permute-start(bf16[512,256]{1,0:T(8,128)(2,1)S(1)} %add_convert_fusion.refs_0_), channel_id=1, source_target_pairs={{0,4},{1,5},{2,6},{3,7},{4,0},{5,1},{6,2},{7,3},{8,12},{9,13},{10,... | collective-permute-start | bytes 786440 | tf_op jit(solution)/shard_map/ppermute | solution.py:445
  168.8 12.8 %collective-permute-start.15 = (bf16[512,256]{1,0:T(8,128)(2,1)S(1)}, bf16[512,256]{1,0:T(8,128)(2,1)}, u32[]{:S(2)}, u32[]{:S(2)}) collective-permute-start(bf16[512,256]{1,0:T(8,128)(2,1)S(1)} %add_convert_fusion.refs_0_), channel_id=1, source_target_pairs={{0,2},{1,3},{2,0},{3,1},{4,6},{5,7},{6,4},{7,5},{8,10},{9,11},{10,... | collective-permute-start | bytes 786440 | tf_op jit(solution)/shard_map/ppermute | solution.py:445
  181.7 25.0 %all-to-all-start.3 = ((bf16[8,256,384]{2,1,0:T(8,128)(2,1)}), bf16[8,256,384]{2,1,0:T(8,128)(2,1)S(1)}, u32[]{:S(2)}, u32[]{:S(2)}) async-start(bf16[8,256,384]{2,1,0:T(8,128)(2,1)} %bitcast.9), calls=%async_computation.3 | async-start | bytes 3145728 | tf_op jit(solution)/shard_map/all_to_all | solution.py:424
  186.2 2.3 %collective-permute-start.19 = (bf16[512,256]{1,0:T(8,128)(2,1)}, bf16[512,256]{1,0:T(8,128)(2,1)S(1)}, u32[]{:S(2)}, u32[]{:S(2)}) collective-permute-start(bf16[512,256]{1,0:T(8,128)(2,1)} %collective-permute-done.15.refs_2_), channel_id=1, source_target_pairs={{0,1},{1,0},{2,3},{3,2},{4,5},{5,4},{6,7},{7,6},{8,9},{9,8},{10,11... | collective-permute-start | bytes 786440 | tf_op jit(solution)/shard_map/ppermute | solution.py:445
  186.3 2.2 %collective-permute-start.20 = (bf16[512,256]{1,0:T(8,128)(2,1)S(1)}, bf16[512,256]{1,0:T(8,128)(2,1)S(1)}, u32[]{:S(2)}, u32[]{:S(2)}) collective-permute-start(bf16[512,256]{1,0:T(8,128)(2,1)S(1)} %copy-done.11), channel_id=1, source_target_pairs={{0,1},{1,0},{2,3},{3,2},{4,5},{5,4},{6,7},{7,6},{8,9},{9,8},{10,11... | collective-permute-start | bytes 786440 | tf_op jit(solution)/shard_map/ppermute | solution.py:445
  (22 other events, 110.3 us)
